TPU v7x, 32 devices: a whole 2x2x4 slice. The times are simulated.
32 devices in a mesh: dp: 8 (over z, y), head: 2 (over x), pos: 2 (over core).
Axes of the slice: x: 2, y: 2, z: 4, core: 2. Of those that a mesh axis runs over, the one named last changes fastest.
Arguments:
- queries: bfloat16 [192, 128, 1024], P('dp', 'pos', 'head'), may hold values from -28 to 28
- output_gradient: bfloat16 [192, 128, 1024], P('dp', 'pos', 'head'), may hold values from -24 to 24
- prefix_keys: bfloat16 [8, 256, 256], P('dp', 'pos', 'head'), may hold values from -12 to 12
- prefix_values: bfloat16 [8, 256, 256], P('dp', 'pos', 'head'), may hold values from -6 to 6
- tile_prefix: int32 [192, 1], replicated, may hold values from 0 to 7; in each aligned block of 24 rows (0 to 23, 24 to 47, ...) at most 3 rows name the same one
- suffix_lse: float32 [192, 128, 8], P(None, None, 'head'), may hold values from 5 to 12
- suffix_dot: float32 [192, 128, 8], P(None, None, 'head'), may hold values from -64 to 64
Outputs:
- query_grad: bfloat16 [192, 128, 1024], P('dp', 'pos', 'head')
- key_grad: bfloat16 [8, 256, 256], P('dp', 'pos', 'head')
- value_grad: bfloat16 [8, 256, 256], P('dp', 'pos', 'head')
Inputs may be any that keep to these rules, and one draw needn't show every extreme that they name: `tile_prefix`: in each aligned block of 24 tiles (the tiles of one dp index) no prefix is named by more than 3 tiles, and some block has a prefix named exactly 3 times.
All inputs are finite; a program needn't handle non-finite values.
Results may differ from a plain program's by a relative error of at most 0.012.
Values may be sent and summed in bfloat16 or wider, within the bound.
A program may use at most 128 MiB of HBM per device.

v0:
```python
import math

import jax
import jax.numpy as jnp
from jax import lax
from jax.sharding import PartitionSpec as P


def joined(value, axis, join):
    pieces = jax.tree.map(lambda part: lax.all_gather(part, axis), value)
    head = jax.tree.map(lambda part: part[0], pieces)
    tail = jax.tree.map(lambda part: part[1:], pieces)
    running, _ = lax.scan(lambda running, piece: (join(running, piece), None), head, tail)
    return running


def block_stats(query_row_set, grad_rows, key_rows, value_rows, scaling):
    scores = (
        jnp.einsum("nd,jd->nj", query_row_set, key_rows, preferred_element_type=jnp.float32)
        * scaling
    )
    prob_grad = jnp.einsum("nd,jd->nj", grad_rows, value_rows, preferred_element_type=jnp.float32)
    row_peak = jnp.max(scores, axis=1)
    shifted = jnp.exp(scores - row_peak[:, None])
    return (row_peak, jnp.sum(shifted, axis=1), jnp.sum(shifted * prob_grad, axis=1))


def block_grads(query_row_set, grad_rows, key_rows, value_rows, row_lse, row_delta, scaling):
    scores = (
        jnp.einsum("nd,jd->nj", query_row_set, key_rows, preferred_element_type=jnp.float32)
        * scaling
    )
    prob_grad = jnp.einsum("nd,jd->nj", grad_rows, value_rows, preferred_element_type=jnp.float32)
    weights = jnp.exp(scores - row_lse[:, None])
    prob_half = weights.astype(jnp.bfloat16)
    score_grad = (weights * (prob_grad - row_delta[:, None])).astype(jnp.bfloat16)
    query_part = jnp.dot(score_grad, key_rows, preferred_element_type=jnp.float32) * scaling
    key_part = (
        jnp.einsum("nj,nd->jd", score_grad, query_row_set, preferred_element_type=jnp.float32)
        * scaling
    )
    value_part = jnp.einsum("nj,nd->jd", prob_half, grad_rows, preferred_element_type=jnp.float32)
    return (query_part, key_part, value_part)


def combine_stats(earlier, later):
    row_peak = jnp.maximum(earlier[0], later[0])
    early_scale = jnp.exp(earlier[0] - row_peak)
    late_scale = jnp.exp(later[0] - row_peak)
    return (
        row_peak,
        earlier[1] * early_scale + later[1] * late_scale,
        earlier[2] * early_scale + later[2] * late_scale,
    )


def finish_stats(row_peak, row_total, row_moment, suffix_l, suffix_d):
    row_top = jnp.maximum(row_peak, suffix_l)
    prefix_part = jnp.exp(row_peak - row_top)
    suffix_part = jnp.exp(suffix_l - row_top)
    row_mass = row_total * prefix_part + suffix_part
    row_lse = row_top + jnp.log(row_mass)
    row_delta = (row_moment * prefix_part + suffix_d * suffix_part) / row_mass
    return (row_lse, row_delta)


def shards(
    queries, output_gradient, prefix_keys, prefix_values, tile_prefix, suffix_lse, suffix_dot
):
    dp_count = lax.axis_size("dp")
    pos_count = lax.axis_size("pos")
    dp_index = lax.axis_index("dp")
    tile_count, row_count, row_width = queries.shape
    head_dim = prefix_keys.shape[2]
    head_count = row_width // head_dim
    tile_rows = row_count * pos_count
    scaling = head_dim ** (-0.5)
    position_limit = max(2, tile_count // dp_count)
    target = tile_prefix[:, 0].reshape(dp_count, tile_count)
    owners = lax.broadcasted_iota(jnp.int32, (1, 1, dp_count), 2)
    onehot = (target[:, :, None] == owners).astype(jnp.int32)
    before = jnp.cumsum(onehot, axis=1) - onehot
    slot_rank = jnp.sum(before * onehot, axis=2)
    own_target = lax.dynamic_index_in_dim(target, dp_index, 0, keepdims=False)
    own_rank = lax.dynamic_index_in_dim(slot_rank, dp_index, 0, keepdims=False)
    dest_ids = lax.broadcasted_iota(jnp.int32, (dp_count, 1, 1), 0)
    slot_ids = lax.broadcasted_iota(jnp.int32, (1, position_limit, 1), 1)
    outgoing_mask = (
        (own_target[None, None, :] == dest_ids) & (own_rank[None, None, :] == slot_ids)
    ).astype(jnp.bfloat16)
    send_query = jnp.einsum(
        "qhb,blo->qhlo", outgoing_mask, queries, preferred_element_type=jnp.float32
    ).astype(jnp.bfloat16)
    send_grad = jnp.einsum(
        "qhb,blo->qhlo", outgoing_mask, output_gradient, preferred_element_type=jnp.float32
    ).astype(jnp.bfloat16)
    came_query, came_grad = (
        lax.all_to_all(send_query, "dp", split_axis=0, concat_axis=0, tiled=True),
        lax.all_to_all(send_grad, "dp", split_axis=0, concat_axis=0, tiled=True),
    )
    source_ids = lax.broadcasted_iota(jnp.int32, (dp_count, 1, 1, 1), 0)
    slot_four = lax.broadcasted_iota(jnp.int32, (1, position_limit, 1, 1), 1)
    block_ids = lax.broadcasted_iota(jnp.int32, (1, 1, dp_count, 1), 2)
    slot_pick = (
        (source_ids == block_ids)
        & (target[None, None] == dp_index)
        & (slot_rank[None, None] == slot_four)
    ).astype(jnp.float32)
    slot_pick = slot_pick.reshape(dp_count * position_limit, dp_count * tile_count)
    slot_lse = jnp.einsum(
        "kt,trh->krh", slot_pick, suffix_lse, precision=lax.Precision.HIGHEST
    ).reshape(dp_count, position_limit, tile_rows, head_count)
    slot_dot = jnp.einsum(
        "kt,trh->krh", slot_pick, suffix_dot, precision=lax.Precision.HIGHEST
    ).reshape(dp_count, position_limit, tile_rows, head_count)
    key_rows = prefix_keys[0]
    value_rows = prefix_values[0]
    all_query, all_grad = (
        lax.all_gather(came_query, "pos", axis=2, tiled=True),
        lax.all_gather(came_grad, "pos", axis=2, tiled=True),
    )
    group_size = math.gcd(dp_count, 8)
    turn_count = dp_count // group_size
    grouped_shape = (turn_count, group_size * position_limit, tile_rows, row_width)
    group_query = all_query.reshape(grouped_shape)
    group_grad = all_grad.reshape(grouped_shape)

    def stats_turn(running, block_list):
        block_query, block_grad = block_list
        stats = block_stats(
            block_query.reshape(-1, head_dim),
            block_grad.reshape(-1, head_dim),
            key_rows,
            value_rows,
            scaling,
        )
        return (running, stats)

    _, partials = lax.scan(stats_turn, jnp.zeros((), jnp.float32), (group_query, group_grad))
    row_peak, row_total, row_moment = joined(partials, "pos", combine_stats)
    flat_shape = (turn_count, group_size * position_limit * tile_rows * head_count)
    row_lse, row_delta = finish_stats(
        row_peak, row_total, row_moment, slot_lse.reshape(flat_shape), slot_dot.reshape(flat_shape)
    )

    def grad_turn(running, pieces):
        block_query, block_grad, block_lse, block_delta = pieces
        query_part, key_part, value_part = block_grads(
            block_query.reshape(-1, head_dim),
            block_grad.reshape(-1, head_dim),
            key_rows,
            value_rows,
            block_lse,
            block_delta,
            scaling,
        )
        return (
            (running[0] + key_part, running[1] + value_part),
            query_part.reshape(group_size * position_limit, tile_rows, row_width),
        )

    zero_sum = jnp.zeros((key_rows.shape[0], head_dim), jnp.float32)
    (key_sum, value_sum), query_all = lax.scan(
        grad_turn, (zero_sum, zero_sum), (group_query, group_grad, row_lse, row_delta)
    )
    query_all = query_all.reshape(dp_count, position_limit, tile_rows, row_width)
    query_mine = lax.psum_scatter(
        query_all.astype(jnp.bfloat16), "pos", scatter_dimension=2, tiled=True
    )
    returned_gradient = lax.all_to_all(query_mine, "dp", split_axis=0, concat_axis=0, tiled=True)
    query_grad = jnp.einsum(
        "byh,byqp->hqp", outgoing_mask, returned_gradient, preferred_element_type=jnp.float32
    ).astype(jnp.bfloat16)
    return (query_grad, key_sum.astype(jnp.bfloat16)[None], value_sum.astype(jnp.bfloat16)[None])


def solution(mesh):
    in_specs = (
        P("dp", "pos", "head"),
        P("dp", "pos", "head"),
        P("dp", "pos", "head"),
        P("dp", "pos", "head"),
        P(),
        P(None, None, "head"),
        P(None, None, "head"),
    )
    out_specs = (P("dp", "pos", "head"), P("dp", "pos", "head"), P("dp", "pos", "head"))
    return jax.shard_map(shards, mesh=mesh, in_specs=in_specs, out_specs=out_specs, check_vma=False)
```

profile of v0, /device:TPU:0, one launch (start us, length us, event | category | flops | bytes accessed | tf_op | source)
XLA Modules:
  0.0 213.0 jit_solution(3336556789177592963)
XLA Ops:
  10.0 3.0 %convolution_convert_fusion.1 = bf16[8,3,64,512]{3,0,2,1:T(8,128)(2,1)S(1)} fusion(bf16[24,64,512]{2,1,0:T(8,128)(2,1)} %param.7, pred[3,24]{1,0:T(4,128)(4,1)S(1)} %iota_compare_fusion.5, pred[8,24]{1,0:T(8,128)(4,1)S(1)} %iota_compare_fusion.4), kind=kOutput, calls=%fused_computation.13 | convolution fusion | flops 38535744 | bytes 3145992 | tf_op jit(solution)/shard_map/qhb,blo->qhlo/dot_general | solution.py:91
  13.5 44.3 %all_to_all.15 = bf16[8,3,64,512]{3,2,1,0:T(8,128)(2,1)} all-to-all(bf16[8,3,64,512]{3,2,1,0:T(8,128)(2,1)S(1)} %copy.62), channel_id=1, replica_groups=mesh['dp'=8,'head'=2,'pos'=2] {'dp'}, dimensions={0} | all-to-all | bytes 3145728 | tf_op jit(solution)/shard_map/all_to_all | solution.py:98
  57.9 1.5 convolution_convert_fusion
  60.0 40.2 %all_to_all.16 = bf16[8,3,64,512]{3,2,1,0:T(8,128)(2,1)} all-to-all(bf16[8,3,64,512]{3,2,1,0:T(8,128)(2,1)S(1)} %copy.67), channel_id=1, replica_groups=mesh['dp'=8,'head'=2,'pos'=2] {'dp'}, dimensions={0} | all-to-all | bytes 3145728 | tf_op jit(solution)/shard_map/all_to_all | solution.py:99
  101.3 1.7 reshape_reshape.6
  103.8 1.7 reshape_reshape.7
  105.5 4.7 %reshape.275 = bf16[12288,128]{1,0:T(8,128)(2,1)S(1)} reshape(bf16[8,3,128,512]{3,2,1,0:T(8,128)(2,1)} %all-gather.6.cloned.1.call-done) | data formatting | bytes 6291456 | tf_op jit(solution)/shard_map/while/body/eval_jaxpr/reshape | solution.py:149
  110.3 4.4 %fusion.44 = (f32[12288]{0:T(1024)S(1)}, f32[12288,128]{0,1:T(8,128)}) fusion(bf16[12288,128]{1,0:T(8,128)(2,1)S(1)} %reshape.275, bf16[1,128,128]{2,1,0:T(8,128)(2,1)} %param.9), kind=kOutput, calls=%fused_computation.72 | convolution fusion | flops 405786624 | bytes 9519104 | tf_op jit(solution)/shard_map/while/body/eval_jaxpr/nd,jd->nj/dot_general | solution.py:30
  115.4 2.0 all-gather
  117.4 4.5 %reshape.276 = bf16[12288,128]{1,0:T(8,128)(2,1)S(1)} reshape(bf16[8,3,128,512]{3,2,1,0:T(8,128)(2,1)} %all-gather.8.cloned.1.call-done) | data formatting | bytes 6291456 | tf_op jit(solution)/shard_map/while/body/eval_jaxpr/reshape | solution.py:150
  121.9 4.8 %fusion.1 = (f32[12288]{0:T(1024)S(1)}, f32[12288]{0:T(1024)S(1)}, f32[12288,128]{0,1:T(8,128)S(1)}) fusion(f32[12288,128]{0,1:T(8,128)} %get-tuple-element.88, f32[12288]{0:T(1024)} %copy-done.3, bf16[12288,128]{1,0:T(8,128)(2,1)S(1)} %reshape.276, bf16[1,128,128]{2,1,0:T(8,128)(2,1)} %param.10), kind=kOutput, calls=%fused_computation.7 | convolution fusion | flops 408920064 | bytes 15908864 | tf_op jit(solution)/shard_map/while/body/eval_jaxpr/nd,jd->nj/dot_general | solution.py:33
  126.8 1.9 all-gather.1
  128.6 2.0 all-gather.2
  130.8 2.8 %multiply_convert_fusion = bf16[12288,128]{0,1:T(8,128)(2,1)} fusion(f32[12288,128]{0,1:T(8,128)S(1)} %get-tuple-element.89, f32[12288,128]{0,1:T(8,128)S(1)} %bitcast.51, f32[12288]{0:T(1024)S(1)} %get-tuple-element.86, f32[12288]{0:T(1024)S(1)} %get-tuple-element.85), kind=kLoop, calls=%fused_computation.3 | loop fusion | flops 6291456 | bytes 15826944 | tf_op jit(solution)/shard_map/while/body/eval_jaxpr/convert_element_type | solution.py:36
  133.6 4.6 %fusion = bf16[12288,128]{0,1:T(8,128)(2,1)} fusion(bf16[12288,128]{0,1:T(8,128)(2,1)} %multiply_convert_fusion, bf16[1,128,128]{2,1,0:T(8,128)(2,1)S(1)} %copy-done.10), kind=kOutput, calls=%fused_computation.2 | convolution fusion | flops 405798912 | bytes 6324224 | tf_op jit(solution)/shard_map/while/body/eval_jaxpr/dot_general | solution.py:37
  138.2 4.7 %copy.71 = bf16[12288,128]{1,0:T(8,128)(2,1)} copy(bf16[12288,128]{0,1:T(8,128)(2,1)} %fusion) | data formatting | bytes 6291456 | tf_op jit(solution)/shard_map/convert_element_type | solution.py:168
  142.9 5.9 %convert_element_type.39 = bf16[8,3,128,512]{3,2,1,0:T(8,128)(2,1)} reshape(bf16[12288,128]{1,0:T(8,128)(2,1)} %copy.71) | data formatting | bytes 6291456 | tf_op jit(solution)/shard_map/convert_element_type | solution.py:168
  148.8 9.9 %reduce-scatter.2.cloned.1.call-done = bf16[8,3,64,512]{3,2,1,0:T(8,128)(2,1)} async-done(((bf16[8,3,128,512]{3,2,1,0:T(8,128)(2,1)}), bf16[8,3,64,512]{3,2,1,0:T(8,128)(2,1)}) %reduce-scatter.2.cloned.1.call-update) | async-done | bytes 1572880 | tf_op jit(solution)/shard_map/reduce_scatter | solution.py:167
  158.8 5.8 %all-to-all-start.2 = ((bf16[8,3,64,512]{3,2,1,0:T(8,128)(2,1)}), bf16[8,3,64,512]{3,2,1,0:T(8,128)(2,1)}, u32[]{:S(2)}, u32[]{:S(2)}) async-start(bf16[8,3,64,512]{3,2,1,0:T(8,128)(2,1)} %reduce-scatter.2.cloned.1.call-done), calls=%async_computation.3 | async-start | bytes 3145728 | tf_op jit(solution)/shard_map/all_to_all | solution.py:170
  164.5 4.4 %fusion.19 = bf16[1,128,128]{2,1,0:T(8,128)(2,1)} fusion(bf16[12288,128]{0,1:T(8,128)(2,1)} %multiply_convert_fusion, bf16[12288,128]{1,0:T(8,128)(2,1)} %copy-done.1), kind=kOutput, calls=%fused_computation.25 | convolution fusion | flops 402685952 | bytes 6324224 | tf_op jit(solution)/shard_map/while/body/eval_jaxpr/nj,nd->jd/dot_general | solution.py:39
  169.0 4.5 %fusion.16 = bf16[1,128,128]{2,1,0:T(8,128)(2,1)} fusion(bf16[12288,128]{1,0:T(8,128)(2,1)S(1)} %reshape.276, f32[12288,128]{0,1:T(8,128)} %get-tuple-element.88, f32[12288]{0:T(1024)S(1)} %copy-done.5), kind=kOutput, calls=%fused_computation.24 | convolution fusion | flops 405815296 | bytes 9519104 | tf_op jit(solution)/shard_map/while/body/eval_jaxpr/nj,nd->jd/dot_general | solution.py:42
  173.5 28.7 %all-to-all-done.2 = bf16[8,3,64,512]{3,2,1,0:T(8,128)(2,1)} async-done(((bf16[8,3,64,512]{3,2,1,0:T(8,128)(2,1)}), bf16[8,3,64,512]{3,2,1,0:T(8,128)(2,1)}, u32[]{:S(2)}, u32[]{:S(2)}) %all-to-all-start.2) | async-done | bytes 1572896 | tf_op jit(solution)/shard_map/all_to_all | solution.py:170
  202.1 2.7 %bitcast_convert_fusion = bf16[24,64,512]{2,0,1:T(8,128)(2,1)S(1)} fusion(bf16[8,3,64,512]{3,2,1,0:T(8,128)(2,1)} %all-to-all-done.2, pred[3,24]{1,0:T(4,128)(4,1)S(1)} %iota_compare_fusion.5, pred[8,24]{1,0:T(8,128)(4,1)S(1)} %iota_compare_fusion.4), kind=kOutput, calls=%fused_computation.10 | convolution fusion | flops 38535744 | bytes 3145992 | tf_op jit(solution)/shard_map/byh,byqp->hqp/dot_general | solution.py:171
  204.9 1.6 copy.73
  (58 shorter events, 6.5 us)
Async XLA Ops:
  7.2 93.4 %copy-start = (f32[192,128,4]{1,2,0:T(4,128)S(1)}, f32[192,128,4]{1,2,0:T(4,128)}, u32[]{:S(2)}) copy-start(f32[192,128,4]{1,2,0:T(4,128)} %param.12) | copy-start | bytes 1179652
  7.2 98.4 %all-gather.6.cloned.1.call-start = ((), (), s32[]{:S(2)}) async-start(), calls=%async_computation.4 | async-start | bytes 4718592 | tf_op jit(solution)/shard_map/all_gather | solution.py:119
  13.5 44.4 %copy-start.2 = (bf16[24,64,512]{2,1,0:T(8,128)(2,1)S(1)}, bf16[24,64,512]{2,1,0:T(8,128)(2,1)}, u32[]{:S(2)}) copy-start(bf16[24,64,512]{2,1,0:T(8,128)(2,1)} %param.8) | copy-start | bytes 4718596
  57.9 59.5 %all-gather.8.cloned.1.call-start = ((), (), s32[]{:S(2)}) async-start(), calls=%async_computation.5 | async-start | bytes 4718592 | tf_op jit(solution)/shard_map/all_gather | solution.py:120
  100.2 2.9 %copy-start.6 = (f32[192,128,4]{1,2,0:T(4,128)S(1)}, f32[192,128,4]{1,2,0:T(4,128)}, u32[]{:S(2)}) copy-start(f32[192,128,4]{1,2,0:T(4,128)} %param.13) | copy-start | bytes 1179652
  100.2 58.6 %reduce-scatter.2.cloned.1.call-start = ((), (), s32[]{:S(2)}) async-start(), calls=%async_computation.6 | async-start | bytes 4718592 | tf_op jit(solution)/shard_map/reduce_scatter | solution.py:167
  110.3 4.4 %copy-start.1 = (bf16[12288,128]{1,0:T(8,128)(2,1)}, bf16[12288,128]{1,0:T(8,128)(2,1)S(1)}, u32[]{:S(2)}) copy-start(bf16[12288,128]{1,0:T(8,128)(2,1)S(1)} %reshape.275) | copy-start | bytes 9437188
  114.7 0.6 copy-start.3
  121.9 8.9 %slice-start = ((s8[6291456]{0:T(1024)(128)(4,1)}), s8[4194304]{0:T(1024)(128)(4,1)S(1)}, s32[]{:S(2)}) async-start(s8[6291456]{0:T(1024)(128)(4,1)} %bitcast.50), calls=%async_computation.7 | async-start | bytes 8388608
  121.9 8.8 %copy-start.7 = (f32[24576]{0:T(1024)S(1)}, f32[24576]{0:T(1024)}, u32[]{:S(2)}) copy-start(f32[24576]{0:T(1024)} %all-gather) | copy-start | bytes 294916
  121.9 8.8 %copy-start.8 = (f32[12288]{0:T(1024)S(1)}, f32[12288]{0:T(1024)}, u32[]{:S(2)}) copy-start(f32[12288]{0:T(1024)} %reshape_reshape.6) | copy-start | bytes 147460
  121.9 8.8 %copy-start.9 = (f32[12288]{0:T(1024)S(1)}, f32[12288]{0:T(1024)}, u32[]{:S(2)}) copy-start(f32[12288]{0:T(1024)} %reshape_reshape.7) | copy-start | bytes 147460
  121.9 8.9 %slice-start.1 = ((s8[6291456]{0:T(1024)(128)(4,1)}), s8[2097152]{0:T(1024)(128)(4,1)S(1)}, s32[]{:S(2)}) async-start(s8[6291456]{0:T(1024)(128)(4,1)} %bitcast.50), calls=%async_computation.8 | async-start | bytes 4194304
  130.8 2.9 %copy-start.4 = (f32[12288]{0:T(1024)}, f32[12288]{0:T(1024)S(1)}, u32[]{:S(2)}) copy-start(f32[12288]{0:T(1024)S(1)} %get-tuple-element.85) | copy-start | bytes 147460
  130.8 2.8 %copy-start.10 = (bf16[1,128,128]{2,1,0:T(8,128)(2,1)S(1)}, bf16[1,128,128]{2,1,0:T(8,128)(2,1)}, u32[]{:S(2)}) copy-start(bf16[1,128,128]{2,1,0:T(8,128)(2,1)} %param.9) | copy-start | bytes 98308
  158.8 43.4 %all-to-all-start.2 = ((bf16[8,3,64,512]{3,2,1,0:T(8,128)(2,1)}), bf16[8,3,64,512]{3,2,1,0:T(8,128)(2,1)}, u32[]{:S(2)}, u32[]{:S(2)}) async-start(bf16[8,3,64,512]{3,2,1,0:T(8,128)(2,1)} %reduce-scatter.2.cloned.1.call-done), calls=%async_computation.3 | async-start | bytes 3145728 | tf_op jit(solution)/shard_map/all_to_all | solution.py:170
  164.5 4.5 %copy-start.5 = (f32[12288]{0:T(1024)S(1)}, f32[12288]{0:T(1024)}, u32[]{:S(2)}) copy-start(f32[12288]{0:T(1024)} %copy-done.4) | copy-start | bytes 147460
Sparse Core Ops, SparseCore 0:
  58.0 11.1 all-gather.5
  100.3 11.0 all-gather.7
  149.0 9.7 reduce-scatter.1
where the time goes:
time: 214 us; the launch traced here: 213 us
  blocking collectives  90.4 us (42%)
  waiting for transfers between devices  38.6 us (18%)
  matrix products  30.5 us (14%)
  local copies, waits for them, and re-layouts  28.7 us (13%)
  between operations  14 us (7%)
  starting transfers between devices  5.88 us (3%)
  other arithmetic  4.92 us (2%)
    all_to_all x1, blocking collectives, shards(): lax.all_to_all(send_query, 'dp', split_axis=0, concat_axis=0, tiled=True)  44.3 us
    all_to_all x1, blocking collectives, shards(): lax.all_to_all(send_grad, 'dp', split_axis=0, concat_axis=0, tiled=True)  40.2 us
    all_to_all x1, waiting for transfers between devices, shards(): lax.all_to_all(query_mine, 'dp', split_axis=0, concat_axis=0, tiled=True)  28.7 us
    convert_element_type x2, local copies, waits for them, and re-layouts, shards(): query_all.astype(jnp.bfloat16)  10.6 us
    reduce_scatter x1, waiting for transfers between devices, shards(): lax.psum_scatter(query_all.astype(jnp.bfloat16), 'pos', scatter_dimension...  9.93 us
    all_gather x3, blocking collectives, joined(): pieces = jax.tree.map(lambda part: lax.all_gather(part, axis), value)  5.92 us
    all_to_all x1, starting transfers between devices, shards(): lax.all_to_all(query_mine, 'dp', split_axis=0, concat_axis=0, tiled=True)  5.76 us
    dot_general x1, matrix products, block_grads(): jnp.einsum('nd,jd->nj', grad_rows, value_rows, preferred_element_type=jnp...  4.84 us
  transfers between devices with their start and end apart: 4, of which 2 were waited for; matrix products, arithmetic and copies ran while one was open for 12% of the time, Pallas kernels for 0%

commit v1 on v0

v1 whole, which is shorter than its diff:
```python
import functools
import math

import jax
import jax.numpy as jnp
from jax import lax
from jax.experimental import pallas as pl
from jax.experimental.pallas import tpu as pltpu
from jax.sharding import PartitionSpec as P

MESH = pl.DeviceIdType.MESH
LOG2E = 1.0 / math.log(2.0)


def exchange_kernel(
    cap,
    q_hbm, g_hbm, k_hbm, v_hbm, tp_ref, lse_hbm, dot_hbm,
    dq_hbm, kg_ref, vg_ref,
    q_ref, g_ref, kv, lse_raw, dot_raw, lse_rows, dot_rows, slots, dq_buf,
    part, sib_out, sib_in, par_out, par_in, line_out, line_in,
    in_sem, kv_recv, kv_sib_send, kv_par_send, kv_line_send,
    sib_send, sib_recv, par_send, par_recv, line_send, line_recv, dq_sem,
):
    tiles, rows, width = q_ref.shape
    prefixes, pos_count, _, block, dim = kv.shape
    heads = width // dim
    line = prefixes // 2
    dp, pos = lax.axis_index("dp"), lax.axis_index("pos")
    a, b = dp // 2, lax.rem(dp, 2)
    other = 1 - b
    scaling = dim ** (-0.5)
    full = cap * prefixes == tiles

    def sibling():
        return {"pos": 1 - pos}

    def partner():
        return {"dp": a * 2 + other}

    def along(d):
        return lax.rem(a + d, line)

    def peer(d):
        return {"dp": along(d) * 2 + b}

    base = dp * tiles
    loads = [
        pltpu.make_async_copy(k_hbm.at[0], kv.at[dp, pos, 0], in_sem.at[0]),
        pltpu.make_async_copy(v_hbm.at[0], kv.at[dp, pos, 1], in_sem.at[1]),
        pltpu.make_async_copy(q_hbm, q_ref, in_sem.at[2]),
        pltpu.make_async_copy(g_hbm, g_ref, in_sem.at[3]),
        pltpu.make_async_copy(lse_hbm.at[pl.ds(base, tiles)], lse_raw, in_sem.at[4]),
        pltpu.make_async_copy(dot_hbm.at[pl.ds(base, tiles)], dot_raw, in_sem.at[5]),
    ]
    for load in loads:
        load.start()

    barrier = pltpu.get_barrier_semaphore()
    pl.semaphore_signal(barrier, inc=1, device_id=sibling(), device_id_type=MESH)
    pl.semaphore_signal(barrier, inc=1, device_id=partner(), device_id_type=MESH)
    for d in range(1, line):
        pl.semaphore_signal(barrier, inc=1, device_id=peer(d), device_id_type=MESH)
    pl.semaphore_wait(barrier, line + 1)

    def remote(src, dst, send, recv, device):
        return pltpu.make_async_remote_copy(
            src_ref=src, dst_ref=dst, send_sem=send, recv_sem=recv,
            device_id=device, device_id_type=MESH,
        )

    def kv_copy(p, send, device):
        mine = kv.at[p, pos]
        return remote(mine, mine, send, kv_recv.at[p, pos], device)

    def kv_wait(p, which):
        here = kv.at[p, which]
        remote(here, here, kv_sib_send.at[p], kv_recv.at[p, which], sibling()).wait_recv()

    loads[0].wait()
    loads[1].wait()
    for d in range(1, line):
        kv_copy(dp, kv_line_send.at[d], peer(d)).start()
    kv_copy(dp, kv_par_send.at[0], partner()).start()
    kv_copy(dp, kv_sib_send.at[dp], sibling()).start()

    def find(p, carry):
        def look(i, found):
            t = tiles - 1 - i
            hit = tp_ref[0, base + t] == p
            shifted = (t,) + found[:-1]
            return tuple(jnp.where(hit, new, old) for new, old in zip(shifted, found))

        found = lax.fori_loop(0, tiles, look, (jnp.int32(-1),) * cap, unroll=True)
        for c in range(cap):
            slots[p * cap + c] = found[c]
        return carry

    lax.fori_loop(0, prefixes, find, 0)

    for load in loads[2:]:
        load.wait()
    for raw, flat in ((lse_raw, lse_rows), (dot_raw, dot_rows)):
        pieces = []
        for h in range(heads):
            row = raw[:, h, :]
            piece = row[:, :rows]
            for other_pos in range(1, pos_count):
                piece = jnp.where(
                    pos == other_pos, row[:, other_pos * rows:(other_pos + 1) * rows], piece
                )
            pieces.append(piece)
        flat[...] = jnp.concatenate(pieces, axis=1)

    def stacked(ref, t):
        tile = ref[t]
        return jnp.concatenate([tile[:, h * dim:(h + 1) * dim] for h in range(heads)], axis=0)

    nt = (((1,), (1,)), ((), ()))
    tn = (((0,), (0,)), ((), ()))
    f32 = jnp.float32

    def compute(p):
        keys = jnp.concatenate([kv[p, i, 0] for i in range(pos_count)], axis=0)
        values = jnp.concatenate([kv[p, i, 1] for i in range(pos_count)], axis=0)
        key_sum = value_sum = None
        for c in range(cap):
            named = slots[p * cap + c]
            t = jnp.maximum(named, 0)
            query, grad = stacked(q_ref, t), stacked(g_ref, t)
            scores = lax.dot_general(keys, query, nt, preferred_element_type=f32)
            prob_grad = lax.dot_general(values, grad, nt, preferred_element_type=f32)
            scores = scores * (scaling * LOG2E)
            suffix_l = lse_rows[pl.ds(t, 1), :] * LOG2E
            suffix_d = dot_rows[pl.ds(t, 1), :]
            top = jnp.maximum(jnp.max(scores, axis=0, keepdims=True), suffix_l)
            shifted = jnp.exp2(scores - top)
            suffix_w = jnp.exp2(suffix_l - top)
            mass = jnp.sum(shifted, axis=0, keepdims=True) + suffix_w
            moment = jnp.sum(shifted * prob_grad, axis=0, keepdims=True) + suffix_w * suffix_d
            inverse = 1.0 / mass
            delta = moment * inverse
            if not full:
                inverse = jnp.where(named >= 0, inverse, 0.0)
            weights = shifted * inverse
            probs = weights.astype(jnp.bfloat16)
            score_grad = (weights * (prob_grad - delta)).astype(jnp.bfloat16)
            key_part = jnp.dot(score_grad, query, preferred_element_type=f32)
            value_part = jnp.dot(probs, grad, preferred_element_type=f32)
            key_sum = key_part if c == 0 else key_sum + key_part
            value_sum = value_part if c == 0 else value_sum + value_part
            query_part = lax.dot_general(score_grad, keys, tn, preferred_element_type=f32)
            query_part = (query_part * scaling).astype(jnp.bfloat16)
            for h in range(heads):
                dq_buf[p, c, :, h * dim:(h + 1) * dim] = query_part[h * rows:(h + 1) * rows]
        key_sum = key_sum * scaling
        for i, total in enumerate((key_sum, value_sum)):
            low, high = total[:block], total[block:]
            part[p, i] = jnp.where(pos == 0, low, high)
            sib_out[p, i] = jnp.where(pos == 0, high, low).astype(jnp.bfloat16)
        remote(
            sib_out.at[p], sib_in.at[p], sib_send.at[p], sib_recv.at[p], sibling()
        ).start()
        pltpu.make_async_copy(dq_buf.at[p], dq_hbm.at[p], dq_sem.at[p]).start()

    def sib_copy(p):
        return remote(sib_out.at[p], sib_in.at[p], sib_send.at[p], sib_recv.at[p], sibling())

    def par_copy(d):
        return remote(par_out.at[d], par_in.at[d], par_send.at[d], par_recv.at[d], partner())

    def line_copy(d):
        return remote(line_out.at[d], line_in.at[d], line_send.at[d], line_recv.at[d], peer(d))

    def to_partner(d):
        p = along(d) * 2 + other
        sib_copy(p).wait_recv()
        par_out[d] = (part[p] + sib_in[p].astype(f32)).astype(jnp.bfloat16)
        par_copy(d).start()

    def chip_sum(d):
        p = along(d) * 2 + b
        sib_copy(p).wait_recv()
        par_copy(d).wait_recv()
        return part[p] + sib_in[p].astype(f32) + par_in[d].astype(f32)

    def to_owner(d):
        line_out[d] = chip_sum(d).astype(jnp.bfloat16)
        line_copy(d).start()

    def turn(d, carry):
        own, across = along(d) * 2 + b, along(d) * 2 + other
        kv_wait(own, 1 - pos)
        compute(own)

        @pl.when(d + 1 < line)
        def _():
            p = along(d + 1) * 2 + b
            kv_wait(p, pos)
            kv_copy(p, kv_par_send.at[d + 1], partner()).start()
            kv_copy(p, kv_sib_send.at[p], sibling()).start()

        @pl.when(d >= 1)
        def _():
            to_partner(d - 1)

        kv_wait(across, pos)
        kv_copy(across, kv_sib_send.at[across], sibling()).start()
        kv_wait(across, 1 - pos)
        compute(across)

        @pl.when(d >= 2)
        def _():
            to_owner(d - 1)

        return carry

    lax.fori_loop(0, line, turn, 0)
    to_partner(line - 1)
    if line > 1:
        to_owner(line - 1)
    total = chip_sum(0)
    for d in range(1, line):
        line_copy(d).wait_recv()
        total = total + line_in[d].astype(f32)
    kg_ref[0] = total[0].astype(jnp.bfloat16)
    vg_ref[0] = total[1].astype(jnp.bfloat16)

    for d in range(1, line):
        kv_copy(dp, kv_line_send.at[d], peer(d)).wait_send()
        line_copy(d).wait_send()

    def drain(d, carry):
        kv_copy(along(d) * 2 + b, kv_par_send.at[d], partner()).wait_send()
        par_copy(d).wait_send()
        return carry

    lax.fori_loop(0, line, drain, 0)

    def drain_prefix(p, carry):
        kv_copy(p, kv_sib_send.at[p], sibling()).wait_send()
        sib_copy(p).wait_send()
        pltpu.make_async_copy(dq_buf.at[p], dq_hbm.at[p], dq_sem.at[p]).wait()
        return carry

    lax.fori_loop(0, prefixes, drain_prefix, 0)


def place_kernel(cap, dq_hbm, kg_hbm, vg_hbm, tp_ref, out_hbm, kg_out, vg_out, counts, sem, small):
    tiles = out_hbm.shape[0]
    prefixes = dq_hbm.shape[0]
    base = lax.axis_index("dp") * tiles
    kg_copy = pltpu.make_async_copy(kg_hbm, kg_out, small.at[0])
    vg_copy = pltpu.make_async_copy(vg_hbm, vg_out, small.at[1])
    kg_copy.start()
    vg_copy.start()
    for p in range(prefixes):
        counts[p] = 0

    def place(t, carry):
        p = tp_ref[0, base + t]
        c = counts[p]
        counts[p] = c + 1
        pltpu.make_async_copy(dq_hbm.at[p, c], out_hbm.at[t], sem.at[t]).start()
        return carry

    def finish(t, carry):
        pltpu.make_async_copy(dq_hbm.at[0, 0], out_hbm.at[t], sem.at[t]).wait()
        return carry

    lax.fori_loop(0, tiles, place, 0)
    lax.fori_loop(0, tiles, finish, 0)
    kg_copy.wait()
    vg_copy.wait()


def shards(
    queries, output_gradient, prefix_keys, prefix_values, tile_prefix, suffix_lse, suffix_dot
):
    prefixes = lax.axis_size("dp")
    pos_count = lax.axis_size("pos")
    tiles, rows, width = queries.shape
    _, block, dim = prefix_keys.shape
    heads = width // dim
    tile_rows = rows * pos_count
    cap = max(2, tiles // prefixes)
    line = prefixes // 2
    bf16, f32 = jnp.bfloat16, jnp.float32
    named = tile_prefix.T
    any_spec = pl.BlockSpec(memory_space=pl.ANY)
    smem_spec = pl.BlockSpec(memory_space=pltpu.SMEM)
    vmem_spec = pl.BlockSpec(memory_space=pltpu.VMEM)
    dma = pltpu.SemaphoreType.DMA
    pair = (2, block, dim)
    work = 10 * tiles * rows * width * block * pos_count
    dq, kg, vg = pl.pallas_call(
        functools.partial(exchange_kernel, cap),
        out_shape=(
            jax.ShapeDtypeStruct((prefixes, cap, rows, width), bf16),
            jax.ShapeDtypeStruct(prefix_keys.shape, bf16),
            jax.ShapeDtypeStruct(prefix_values.shape, bf16),
        ),
        in_specs=[any_spec] * 4 + [smem_spec] + [any_spec] * 2,
        out_specs=(any_spec, vmem_spec, vmem_spec),
        scratch_shapes=[
            pltpu.VMEM((tiles, rows, width), bf16),
            pltpu.VMEM((tiles, rows, width), bf16),
            pltpu.VMEM((prefixes, pos_count) + pair, bf16),
            pltpu.VMEM((tiles, heads, tile_rows), f32),
            pltpu.VMEM((tiles, heads, tile_rows), f32),
            pltpu.VMEM((tiles, heads * rows), f32),
            pltpu.VMEM((tiles, heads * rows), f32),
            pltpu.SMEM((prefixes * cap,), jnp.int32),
            pltpu.VMEM((prefixes, cap, rows, width), bf16),
            pltpu.VMEM((prefixes,) + pair, f32),
            pltpu.VMEM((prefixes,) + pair, bf16),
            pltpu.VMEM((prefixes,) + pair, bf16),
            pltpu.VMEM((line,) + pair, bf16),
            pltpu.VMEM((line,) + pair, bf16),
            pltpu.VMEM((line,) + pair, bf16),
            pltpu.VMEM((line,) + pair, bf16),
            dma((6,)),
            dma((prefixes, pos_count)),
            dma((prefixes,)),
            dma((line,)),
            dma((line,)),
            dma((prefixes,)),
            dma((prefixes,)),
            dma((line,)),
            dma((line,)),
            dma((line,)),
            dma((line,)),
            dma((prefixes,)),
        ],
        compiler_params=pltpu.CompilerParams(
            collective_id=0, has_side_effects=True, vmem_limit_bytes=48 << 20
        ),
        cost_estimate=pl.CostEstimate(
            flops=work, bytes_accessed=6 * tiles * rows * width, transcendentals=0
        ),
        name="prefix_grads",
    )(
        queries, output_gradient, prefix_keys, prefix_values, named,
        jnp.swapaxes(suffix_lse, 1, 2), jnp.swapaxes(suffix_dot, 1, 2),
    )
    return pl.pallas_call(
        functools.partial(place_kernel, cap),
        out_shape=(
            jax.ShapeDtypeStruct(queries.shape, bf16),
            jax.ShapeDtypeStruct(prefix_keys.shape, bf16),
            jax.ShapeDtypeStruct(prefix_values.shape, bf16),
        ),
        in_specs=[any_spec] * 3 + [smem_spec],
        out_specs=(any_spec,) * 3,
        scratch_shapes=[pltpu.SMEM((prefixes,), jnp.int32), dma((tiles,)), dma((2,))],
        name="place_tiles",
    )(dq, kg, vg, named)


def solution(mesh):
    in_specs = (
        P("dp", "pos", "head"),
        P("dp", "pos", "head"),
        P("dp", "pos", "head"),
        P("dp", "pos", "head"),
        P(),
        P(None, None, "head"),
        P(None, None, "head"),
    )
    out_specs = (P("dp", "pos", "head"), P("dp", "pos", "head"), P("dp", "pos", "head"))
    return jax.shard_map(shards, mesh=mesh, in_specs=in_specs, out_specs=out_specs, check_vma=False)
```

time: 214 us -> 100 us (0.47)
  blocking collectives: 90.4 us -> 0 us
  Pallas kernels: 0 us -> 89.5 us
  waiting for transfers between devices: 38.6 us -> 0 us
  matrix products: 30.5 us -> 0 us
  local copies, waits for them, and re-layouts: 28.7 us -> 9.37 us
  between operations: 14 us -> 0.67 us
  starting transfers between devices: 5.88 us -> 0 us
  other arithmetic: 4.92 us -> 0 us
    pallas_call x0 -> x2, Pallas kernels: none -> 89.5 us  [the longest x1 51.7 us: shards(): pl.pallas_call(functools.partial(place_kernel, cap), out_shape=(jax.Shape...]
    all_to_all x2 -> x0, blocking collectives: 84.5 us -> none  [the longest x1 44.3 us: shards(): lax.all_to_all(send_query, 'dp', split_axis=0, concat_axis=0, tiled=True)]
    dot_general x10 -> x0, matrix products: 30.5 us -> none  [the longest x1 4.84 us: block_grads(): jnp.einsum('nd,jd->nj', grad_rows, value_rows, preferred_element_type=jnp...]
    all_to_all x1 -> x0, waiting for transfers between devices: 28.7 us -> none  [shards(): lax.all_to_all(query_mine, 'dp', split_axis=0, concat_axis=0, tiled=True)]
    convert_element_type x4 -> x0, local copies, waits for them, and re-layouts: 11.6 us -> none  [the longest x2 10.6 us: shards(): query_all.astype(jnp.bfloat16)]
    reduce_scatter x1 -> x0, waiting for transfers between devices: 9.93 us -> none  [shards(): lax.psum_scatter(query_all.astype(jnp.bfloat16), 'pos', scatter_dimension...]
    reshape x2 -> x0, local copies, waits for them, and re-layouts: 9.24 us -> none  [the longest x1 4.74 us: grad_turn(): block_query.reshape(-1, head_dim)]
    unnamed x28 -> x20, local copies, waits for them, and re-layouts: 2.84 us -> 9.37 us
  transfers between devices with their start and end apart: 4 -> 0, of which waited for: 2 -> 0; matrix products, arithmetic and copies ran while one was open for 12% -> 0% of each run, Pallas kernels for 0% -> 0%
where the time goes in v1:
time: 100 us; the launch traced here: 99.6 us
  Pallas kernels  89.5 us (90%)
  local copies, waits for them, and re-layouts  9.37 us (9%)
    pallas_call x1, Pallas kernels, shards(): pl.pallas_call(functools.partial(place_kernel, cap), out_shape=(jax.Shape...  51.7 us
    pallas_call x1, Pallas kernels, shards(): pl.pallas_call(functools.partial(exchange_kernel, cap), out_shape=(jax.Sh...  37.9 us
    unnamed x20, local copies, waits for them, and re-layouts  9.37 us

profile of v1, /device:TPU:0, one launch (start us, length us, event | category | flops | bytes accessed | tf_op | source)
XLA Modules:
  0.0 99.6 jit_solution(18432451376971014603)
XLA Ops:
  0.6 0.0 copy-start.3
  0.6 0.7 copy-done.3
  1.3 0.0 copy-start.4
  1.3 1.4 %copy-done.4 = bf16[24,64,512]{2,1,0:T(8,128)(2,1)S(1)} copy-done((bf16[24,64,512]{2,1,0:T(8,128)(2,1)S(1)}, bf16[24,64,512]{2,1,0:T(8,128)(2,1)}, u32[]{:S(2)}) %copy-start.4) | copy-done | bytes 1572888
  2.7 0.0 copy-start.5
  2.7 1.4 %copy-done.5 = bf16[24,64,512]{2,1,0:T(8,128)(2,1)S(1)} copy-done((bf16[24,64,512]{2,1,0:T(8,128)(2,1)S(1)}, bf16[24,64,512]{2,1,0:T(8,128)(2,1)}, u32[]{:S(2)}) %copy-start.5) | copy-done | bytes 1572888
  4.1 0.0 copy-start.6
  4.1 1.0 copy-done.6
  5.1 0.0 copy-start.7
  5.1 1.0 copy-done.7
  6.1 0.0 copy-start.8
  6.1 0.8 copy-done.8
  6.9 0.0 copy-start.9
  6.9 0.8 copy-done.9
  7.6 37.9 %prefix_grads.1 = (bf16[8,3,64,512]{3,2,1,0:T(8,128)(2,1)S(1)}, bf16[1,128,128]{2,1,0:T(8,128)(2,1)S(1)}, bf16[1,128,128]{2,1,0:T(8,128)(2,1)S(1)}) custom-call(bf16[24,64,512]{2,1,0:T(8,128)(2,1)S(1)} %copy-done.4, bf16[24,64,512]{2,1,0:T(8,128)(2,1)S(1)} %copy-done.5, bf16[1,128,128]{2,1,0:T(8,128)(2,1)S(1)} %copy-done.8, ...), custom_call_target="tpu_custom_call" | custom-call | flops 2013265920 | bytes 4718592 | tf_op jit(solution)/shard_map/prefix_grads/pallas_call | solution.py:295
  45.5 0.0 copy-start
  45.6 1.1 %copy-done = bf16[8,3,64,512]{3,2,1,0:T(8,128)(2,1)} copy-done((bf16[8,3,64,512]{3,2,1,0:T(8,128)(2,1)}, bf16[8,3,64,512]{3,2,1,0:T(8,128)(2,1)S(1)}, u32[]{:S(2)}) %copy-start) | copy-done | bytes 1572888
  46.7 0.0 copy-start.1
  46.7 0.6 copy-done.1
  47.3 0.0 copy-start.2
  47.3 0.6 copy-done.2
  47.9 51.7 %place_tiles.1 = (bf16[24,64,512]{2,1,0:T(8,128)(2,1)}, bf16[1,128,128]{2,1,0:T(8,128)(2,1)}, bf16[1,128,128]{2,1,0:T(8,128)(2,1)}) custom-call(bf16[8,3,64,512]{3,2,1,0:T(8,128)(2,1)} %copy-done, bf16[1,128,128]{2,1,0:T(8,128)(2,1)} %copy-done.1, bf16[1,128,128]{2,1,0:T(8,128)(2,1)} %copy-done.2, s32[1,192]{1,0:T(1,128)} %bitcast.3), custom_call_target="tpu_custom_call" | custom-call | tf_op jit(solution)/shard_map/place_tiles/pallas_call | solution.py:345
Async XLA Ops:
  0.6 0.7 copy-start.3
  1.3 1.4 %copy-start.4 = (bf16[24,64,512]{2,1,0:T(8,128)(2,1)S(1)}, bf16[24,64,512]{2,1,0:T(8,128)(2,1)}, u32[]{:S(2)}) copy-start(bf16[24,64,512]{2,1,0:T(8,128)(2,1)} %q_hbm.1) | copy-start | bytes 4718596
  2.7 1.4 %copy-start.5 = (bf16[24,64,512]{2,1,0:T(8,128)(2,1)S(1)}, bf16[24,64,512]{2,1,0:T(8,128)(2,1)}, u32[]{:S(2)}) copy-start(bf16[24,64,512]{2,1,0:T(8,128)(2,1)} %g_hbm.1) | copy-start | bytes 4718596
  4.1 1.0 copy-start.6
  5.1 1.0 copy-start.7
  6.1 0.8 copy-start.8
  6.9 0.8 copy-start.9
  45.5 1.2 %copy-start = (bf16[8,3,64,512]{3,2,1,0:T(8,128)(2,1)}, bf16[8,3,64,512]{3,2,1,0:T(8,128)(2,1)S(1)}, u32[]{:S(2)}) copy-start(bf16[8,3,64,512]{3,2,1,0:T(8,128)(2,1)S(1)} %get-tuple-element.6.dq_hbm) | copy-start | bytes 4718596
  46.7 0.6 copy-start.1
  47.3 0.6 copy-start.2

commit v2 on v1

--- a/solution.py
+++ b/solution.py
@@ -14,12 +14,12 @@
 
 def exchange_kernel(
     cap,
-    q_hbm, g_hbm, k_hbm, v_hbm, tp_ref, lse_hbm, dot_hbm,
-    dq_hbm, kg_ref, vg_ref,
-    q_ref, g_ref, kv, lse_raw, dot_raw, lse_rows, dot_rows, slots, dq_buf,
+    q_hbm, g_hbm, k_hbm, v_hbm, tp_hbm, lse_hbm, dot_hbm,
+    dq_ref, kg_ref, vg_ref,
+    tp_ref, q_ref, g_ref, kv, lse_raw, dot_raw, lse_rows, dot_rows, slots,
     part, sib_out, sib_in, par_out, par_in, line_out, line_in,
     in_sem, kv_recv, kv_sib_send, kv_par_send, kv_line_send,
-    sib_send, sib_recv, par_send, par_recv, line_send, line_recv, dq_sem,
+    sib_send, sib_recv, par_send, par_recv, line_send, line_recv,
 ):
     tiles, rows, width = q_ref.shape
     prefixes, pos_count, _, block, dim = kv.shape
@@ -51,6 +51,7 @@
         pltpu.make_async_copy(g_hbm, g_ref, in_sem.at[3]),
         pltpu.make_async_copy(lse_hbm.at[pl.ds(base, tiles)], lse_raw, in_sem.at[4]),
         pltpu.make_async_copy(dot_hbm.at[pl.ds(base, tiles)], dot_raw, in_sem.at[5]),
+        pltpu.make_async_copy(tp_hbm, tp_ref, in_sem.at[6]),
     ]
     for load in loads:
         load.start()
@@ -83,6 +84,8 @@
     kv_copy(dp, kv_par_send.at[0], partner()).start()
     kv_copy(dp, kv_sib_send.at[dp], sibling()).start()
 
+    loads[6].wait()
+
     def find(p, carry):
         def look(i, found):
             t = tiles - 1 - i
@@ -97,7 +100,7 @@
 
     lax.fori_loop(0, prefixes, find, 0)
 
-    for load in loads[2:]:
+    for load in loads[2:6]:
         load.wait()
     for raw, flat in ((lse_raw, lse_rows), (dot_raw, dot_rows)):
         pieces = []
@@ -116,12 +119,12 @@
         return jnp.concatenate([tile[:, h * dim:(h + 1) * dim] for h in range(heads)], axis=0)
 
     nt = (((1,), (1,)), ((), ()))
-    tn = (((0,), (0,)), ((), ()))
     f32 = jnp.float32
 
     def compute(p):
         keys = jnp.concatenate([kv[p, i, 0] for i in range(pos_count)], axis=0)
         values = jnp.concatenate([kv[p, i, 1] for i in range(pos_count)], axis=0)
+        keys_t = keys.T
         key_sum = value_sum = None
         for c in range(cap):
             named = slots[p * cap + c]
@@ -148,10 +151,10 @@
             value_part = jnp.dot(probs, grad, preferred_element_type=f32)
             key_sum = key_part if c == 0 else key_sum + key_part
             value_sum = value_part if c == 0 else value_sum + value_part
-            query_part = lax.dot_general(score_grad, keys, tn, preferred_element_type=f32)
-            query_part = (query_part * scaling).astype(jnp.bfloat16)
+            query_part = jnp.dot(keys_t, score_grad, preferred_element_type=f32)
+            query_part = (query_part * scaling).T.astype(jnp.bfloat16)
             for h in range(heads):
-                dq_buf[p, c, :, h * dim:(h + 1) * dim] = query_part[h * rows:(h + 1) * rows]
+                dq_ref[p, c, :, h * dim:(h + 1) * dim] = query_part[h * rows:(h + 1) * rows]
         key_sum = key_sum * scaling
         for i, total in enumerate((key_sum, value_sum)):
             low, high = total[:block], total[block:]
@@ -160,7 +163,6 @@
         remote(
             sib_out.at[p], sib_in.at[p], sib_send.at[p], sib_recv.at[p], sibling()
         ).start()
-        pltpu.make_async_copy(dq_buf.at[p], dq_hbm.at[p], dq_sem.at[p]).start()
 
     def sib_copy(p):
         return remote(sib_out.at[p], sib_in.at[p], sib_send.at[p], sib_recv.at[p], sibling())
@@ -239,18 +241,17 @@
     def drain_prefix(p, carry):
         kv_copy(p, kv_sib_send.at[p], sibling()).wait_send()
         sib_copy(p).wait_send()
-        pltpu.make_async_copy(dq_buf.at[p], dq_hbm.at[p], dq_sem.at[p]).wait()
         return carry
 
     lax.fori_loop(0, prefixes, drain_prefix, 0)
 
 
-def place_kernel(cap, dq_hbm, kg_hbm, vg_hbm, tp_ref, out_hbm, kg_out, vg_out, counts, sem, small):
+def place_kernel(cap, dq_ref, kg_ref, vg_ref, tp_ref, out_hbm, kg_out, vg_out, counts, sem, small):
     tiles = out_hbm.shape[0]
-    prefixes = dq_hbm.shape[0]
+    prefixes = dq_ref.shape[0]
     base = lax.axis_index("dp") * tiles
-    kg_copy = pltpu.make_async_copy(kg_hbm, kg_out, small.at[0])
-    vg_copy = pltpu.make_async_copy(vg_hbm, vg_out, small.at[1])
+    kg_copy = pltpu.make_async_copy(kg_ref, kg_out, small.at[0])
+    vg_copy = pltpu.make_async_copy(vg_ref, vg_out, small.at[1])
     kg_copy.start()
     vg_copy.start()
     for p in range(prefixes):
@@ -260,17 +261,21 @@
         p = tp_ref[0, base + t]
         c = counts[p]
         counts[p] = c + 1
-        pltpu.make_async_copy(dq_hbm.at[p, c], out_hbm.at[t], sem.at[t]).start()
+        pltpu.make_async_copy(dq_ref.at[p, c], out_hbm.at[t], sem.at[t]).start()
         return carry
 
     def finish(t, carry):
-        pltpu.make_async_copy(dq_hbm.at[0, 0], out_hbm.at[t], sem.at[t]).wait()
+        pltpu.make_async_copy(dq_ref.at[0, 0], out_hbm.at[t], sem.at[t]).wait()
         return carry
 
     lax.fori_loop(0, tiles, place, 0)
     lax.fori_loop(0, tiles, finish, 0)
     kg_copy.wait()
     vg_copy.wait()
+
+
+def stay(array):
+    return pltpu.with_memory_space_constraint(array, pltpu.HBM)
 
 
 def shards(
@@ -285,8 +290,8 @@
     cap = max(2, tiles // prefixes)
     line = prefixes // 2
     bf16, f32 = jnp.bfloat16, jnp.float32
-    named = tile_prefix.T
-    any_spec = pl.BlockSpec(memory_space=pl.ANY)
+    named = stay(tile_prefix.T)
+    hbm_spec = pl.BlockSpec(memory_space=pltpu.HBM)
     smem_spec = pl.BlockSpec(memory_space=pltpu.SMEM)
     vmem_spec = pl.BlockSpec(memory_space=pltpu.VMEM)
     dma = pltpu.SemaphoreType.DMA
@@ -299,9 +304,10 @@
             jax.ShapeDtypeStruct(prefix_keys.shape, bf16),
             jax.ShapeDtypeStruct(prefix_values.shape, bf16),
         ),
-        in_specs=[any_spec] * 4 + [smem_spec] + [any_spec] * 2,
-        out_specs=(any_spec, vmem_spec, vmem_spec),
+        in_specs=[hbm_spec] * 7,
+        out_specs=(vmem_spec, vmem_spec, vmem_spec),
         scratch_shapes=[
+            pltpu.SMEM(named.shape, jnp.int32),
             pltpu.VMEM((tiles, rows, width), bf16),
             pltpu.VMEM((tiles, rows, width), bf16),
             pltpu.VMEM((prefixes, pos_count) + pair, bf16),
@@ -310,7 +316,6 @@
             pltpu.VMEM((tiles, heads * rows), f32),
             pltpu.VMEM((tiles, heads * rows), f32),
             pltpu.SMEM((prefixes * cap,), jnp.int32),
-            pltpu.VMEM((prefixes, cap, rows, width), bf16),
             pltpu.VMEM((prefixes,) + pair, f32),
             pltpu.VMEM((prefixes,) + pair, bf16),
             pltpu.VMEM((prefixes,) + pair, bf16),
@@ -318,7 +323,7 @@
             pltpu.VMEM((line,) + pair, bf16),
             pltpu.VMEM((line,) + pair, bf16),
             pltpu.VMEM((line,) + pair, bf16),
-            dma((6,)),
+            dma((7,)),
             dma((prefixes, pos_count)),
             dma((prefixes,)),
             dma((line,)),
@@ -329,7 +334,6 @@
             dma((line,)),
             dma((line,)),
             dma((line,)),
-            dma((prefixes,)),
         ],
         compiler_params=pltpu.CompilerParams(
             collective_id=0, has_side_effects=True, vmem_limit_bytes=48 << 20
@@ -339,8 +343,8 @@
         ),
         name="prefix_grads",
     )(
-        queries, output_gradient, prefix_keys, prefix_values, named,
-        jnp.swapaxes(suffix_lse, 1, 2), jnp.swapaxes(suffix_dot, 1, 2),
+        stay(queries), stay(output_gradient), stay(prefix_keys), stay(prefix_values), named,
+        stay(jnp.swapaxes(suffix_lse, 1, 2)), stay(jnp.swapaxes(suffix_dot, 1, 2)),
     )
     return pl.pallas_call(
         functools.partial(place_kernel, cap),
@@ -349,9 +353,10 @@
             jax.ShapeDtypeStruct(prefix_keys.shape, bf16),
             jax.ShapeDtypeStruct(prefix_values.shape, bf16),
         ),
-        in_specs=[any_spec] * 3 + [smem_spec],
-        out_specs=(any_spec,) * 3,
+        in_specs=[vmem_spec] * 3 + [smem_spec],
+        out_specs=(hbm_spec,) * 3,
         scratch_shapes=[pltpu.SMEM((prefixes,), jnp.int32), dma((tiles,)), dma((2,))],
+        compiler_params=pltpu.CompilerParams(vmem_limit_bytes=16 << 20),
         name="place_tiles",
     )(dq, kg, vg, named)
 

time: 100 us -> 38.6 us (0.39)
  Pallas kernels: 89.5 us -> 37.8 us
  local copies, waits for them, and re-layouts: 9.37 us -> 0 us
    pallas_call x1, Pallas kernels: 51.7 us -> 2.06 us  [shards(): pl.pallas_call(functools.partial(place_kernel, cap), out_shape=(jax.Shape...]
    unnamed x20 -> x0, local copies, waits for them, and re-layouts: 9.37 us -> none
    pallas_call x1, Pallas kernels: 37.9 us -> 35.7 us  [shards(): pl.pallas_call(functools.partial(exchange_kernel, cap), out_shape=(jax.Sh...]
where the time goes in v2:
time: 38.6 us; the launch traced here: 38.4 us
  Pallas kernels  37.8 us (98%)
  between operations  0.64 us (2%)
    pallas_call x1, Pallas kernels, shards(): pl.pallas_call(functools.partial(exchange_kernel, cap), out_shape=(jax.Sh...  35.7 us
    pallas_call x1, Pallas kernels, shards(): pl.pallas_call(functools.partial(place_kernel, cap), out_shape=(jax.Shape...  2.06 us

profile of v2, /device:TPU:0, one launch (start us, length us, event | category | flops | bytes accessed | tf_op | source)
XLA Modules:
  0.0 38.4 jit_solution(10420492332481583292)
XLA Ops:
  0.6 35.7 %prefix_grads.1 = (bf16[8,3,64,512]{3,2,1,0:T(8,128)(2,1)S(1)}, bf16[1,128,128]{2,1,0:T(8,128)(2,1)S(1)}, bf16[1,128,128]{2,1,0:T(8,128)(2,1)S(1)}) custom-call(bf16[24,64,512]{2,1,0:T(8,128)(2,1)} %q_hbm.1, bf16[24,64,512]{2,1,0:T(8,128)(2,1)} %g_hbm.1, bf16[1,128,128]{2,1,0:T(8,128)(2,1)} %k_hbm.1, bf16[1,128,128]{2,1,0:T(8,128)(2,1)} %v_hbm.1, ...), custom_call_target="tpu_custom_call" | custom-call | flops 2013265920 | bytes 4718592 | tf_op jit(solution)/shard_map/prefix_grads/pallas_call | solution.py:300
  36.4 2.1 %place_tiles.1 = (bf16[24,64,512]{2,1,0:T(8,128)(2,1)}, bf16[1,128,128]{2,1,0:T(8,128)(2,1)}, bf16[1,128,128]{2,1,0:T(8,128)(2,1)}) custom-call(bf16[8,3,64,512]{3,2,1,0:T(8,128)(2,1)S(1)} %get-tuple-element.6.dq_ref, bf16[1,128,128]{2,1,0:T(8,128)(2,1)S(1)} %get-tuple-element.7.kg_ref, bf16[1,128,128]{2,1,0:T(8,128)(2,1)S(1)} %get-tuple-element.8.vg_ref, ...), custom_call_target="tpu_custom_call" | custom-call | tf_op jit(solution)/shard_map/place_tiles/pallas_call | solution.py:349

commit v3 on v2

--- a/solution.py
+++ b/solution.py
@@ -124,17 +124,17 @@
     def compute(p):
         keys = jnp.concatenate([kv[p, i, 0] for i in range(pos_count)], axis=0)
         values = jnp.concatenate([kv[p, i, 1] for i in range(pos_count)], axis=0)
-        keys_t = keys.T
-        key_sum = value_sum = None
+        named = [slots[p * cap + c] for c in range(cap)]
+        found = [jnp.maximum(t, 0) for t in named]
+        query = [stacked(q_ref, t) for t in found]
+        grad = [stacked(g_ref, t) for t in found]
+        probs, score_grad = [], []
         for c in range(cap):
-            named = slots[p * cap + c]
-            t = jnp.maximum(named, 0)
-            query, grad = stacked(q_ref, t), stacked(g_ref, t)
-            scores = lax.dot_general(keys, query, nt, preferred_element_type=f32)
-            prob_grad = lax.dot_general(values, grad, nt, preferred_element_type=f32)
+            scores = lax.dot_general(keys, query[c], nt, preferred_element_type=f32)
+            prob_grad = lax.dot_general(values, grad[c], nt, preferred_element_type=f32)
+            suffix_l = lse_rows[pl.ds(found[c], 1), :] * LOG2E
+            suffix_d = dot_rows[pl.ds(found[c], 1), :]
             scores = scores * (scaling * LOG2E)
-            suffix_l = lse_rows[pl.ds(t, 1), :] * LOG2E
-            suffix_d = dot_rows[pl.ds(t, 1), :]
             top = jnp.maximum(jnp.max(scores, axis=0, keepdims=True), suffix_l)
             shifted = jnp.exp2(scores - top)
             suffix_w = jnp.exp2(suffix_l - top)
@@ -143,18 +143,14 @@
             inverse = 1.0 / mass
             delta = moment * inverse
             if not full:
-                inverse = jnp.where(named >= 0, inverse, 0.0)
+                inverse = jnp.where(named[c] >= 0, inverse, 0.0)
             weights = shifted * inverse
-            probs = weights.astype(jnp.bfloat16)
-            score_grad = (weights * (prob_grad - delta)).astype(jnp.bfloat16)
-            key_part = jnp.dot(score_grad, query, preferred_element_type=f32)
-            value_part = jnp.dot(probs, grad, preferred_element_type=f32)
-            key_sum = key_part if c == 0 else key_sum + key_part
-            value_sum = value_part if c == 0 else value_sum + value_part
-            query_part = jnp.dot(keys_t, score_grad, preferred_element_type=f32)
-            query_part = (query_part * scaling).T.astype(jnp.bfloat16)
-            for h in range(heads):
-                dq_ref[p, c, :, h * dim:(h + 1) * dim] = query_part[h * rows:(h + 1) * rows]
+            probs.append(weights.astype(jnp.bfloat16))
+            score_grad.append((weights * (prob_grad - delta)).astype(jnp.bfloat16))
+        probs = jnp.concatenate(probs, axis=1)
+        score_grad = jnp.concatenate(score_grad, axis=1)
+        value_sum = jnp.dot(probs, jnp.concatenate(grad, axis=0), preferred_element_type=f32)
+        key_sum = jnp.dot(score_grad, jnp.concatenate(query, axis=0), preferred_element_type=f32)
         key_sum = key_sum * scaling
         for i, total in enumerate((key_sum, value_sum)):
             low, high = total[:block], total[block:]
@@ -163,6 +159,12 @@
         remote(
             sib_out.at[p], sib_in.at[p], sib_send.at[p], sib_recv.at[p], sibling()
         ).start()
+        query_part = jnp.dot(keys.T, score_grad, preferred_element_type=f32)
+        query_part = (query_part * scaling).astype(jnp.bfloat16).T
+        for c in range(cap):
+            for h in range(heads):
+                first = (c * heads + h) * rows
+                dq_ref[p, c, :, h * dim:(h + 1) * dim] = query_part[first:first + rows]
 
     def sib_copy(p):
         return remote(sib_out.at[p], sib_in.at[p], sib_send.at[p], sib_recv.at[p], sibling())
@@ -189,35 +191,51 @@
         line_out[d] = chip_sum(d).astype(jnp.bfloat16)
         line_copy(d).start()
 
-    def turn(d, carry):
-        own, across = along(d) * 2 + b, along(d) * 2 + other
-        kv_wait(own, 1 - pos)
-        compute(own)
-
-        @pl.when(d + 1 < line)
-        def _():
-            p = along(d + 1) * 2 + b
-            kv_wait(p, pos)
-            kv_copy(p, kv_par_send.at[d + 1], partner()).start()
-            kv_copy(p, kv_sib_send.at[p], sibling()).start()
-
-        @pl.when(d >= 1)
-        def _():
-            to_partner(d - 1)
-
-        kv_wait(across, pos)
-        kv_copy(across, kv_sib_send.at[across], sibling()).start()
-        kv_wait(across, 1 - pos)
-        compute(across)
-
-        @pl.when(d >= 2)
-        def _():
-            to_owner(d - 1)
-
-        return carry
-
-    lax.fori_loop(0, line, turn, 0)
-    to_partner(line - 1)
+    def forward_along(d):
+        p = along(d) * 2 + b
+        kv_wait(p, pos)
+        kv_copy(p, kv_par_send.at[d], partner()).start()
+        kv_copy(p, kv_sib_send.at[p], sibling()).start()
+
+    def forward_across(d):
+        p = along(d) * 2 + other
+        kv_wait(p, pos)
+        kv_copy(p, kv_sib_send.at[p], sibling()).start()
+
+    def step(s, carry):
+        half = (s + 1) // 2
+        odd = lax.rem(s, 2) == 1
+        across = ((s > 0) & (lax.rem(s, 2) == 0)) | (s == 2 * line - 1)
+        p = along(lax.rem(half, line)) * 2 + jnp.where(across, other, b)
+        kv_wait(p, 1 - pos)
+        compute(p)
+
+        @pl.when(s == 0)
+        def _():
+            if line > 1:
+                forward_along(1)
+            forward_across(0)
+
+        @pl.when(odd & (half + 1 < line))
+        def _():
+            forward_along(half + 1)
+
+        @pl.when(odd & (half < line))
+        def _():
+            forward_across(half)
+
+        @pl.when(odd & (s >= 3))
+        def _():
+            to_partner(half - 1)
+
+        @pl.when((lax.rem(s, 2) == 0) & (s >= 4))
+        def _():
+            to_owner(half - 1)
+
+        return carry
+
+    lax.fori_loop(0, 2 * line, step, 0)
+    to_partner(0)
     if line > 1:
         to_owner(line - 1)
     total = chip_sum(0)

time: 38.6 us -> 38 us (0.984)
  Pallas kernels: 37.8 us -> 37.2 us
    pallas_call x1, Pallas kernels: 35.7 us -> 35.2 us  [shards(): pl.pallas_call(functools.partial(exchange_kernel, cap), out_shape=(jax.Sh...]
where the time goes in v3:
time: 38 us; the launch traced here: 37.9 us
  Pallas kernels  37.2 us (98%)
  between operations  0.64 us (2%)
    pallas_call x1, Pallas kernels, shards(): pl.pallas_call(functools.partial(exchange_kernel, cap), out_shape=(jax.Sh...  35.2 us
    pallas_call x1, Pallas kernels, shards(): pl.pallas_call(functools.partial(place_kernel, cap), out_shape=(jax.Shape...  2.06 us

profile of v3, /device:TPU:0, one launch (start us, length us, event | category | flops | bytes accessed | tf_op | source)
XLA Modules:
  0.0 37.9 jit_solution(14376635214738209866)
XLA Ops:
  0.6 35.2 %prefix_grads.1 = (bf16[8,3,64,512]{3,2,1,0:T(8,128)(2,1)S(1)}, bf16[1,128,128]{2,1,0:T(8,128)(2,1)S(1)}, bf16[1,128,128]{2,1,0:T(8,128)(2,1)S(1)}) custom-call(bf16[24,64,512]{2,1,0:T(8,128)(2,1)} %q_hbm.1, bf16[24,64,512]{2,1,0:T(8,128)(2,1)} %g_hbm.1, bf16[1,128,128]{2,1,0:T(8,128)(2,1)} %k_hbm.1, bf16[1,128,128]{2,1,0:T(8,128)(2,1)} %v_hbm.1, ...), custom_call_target="tpu_custom_call" | custom-call | flops 2013265920 | bytes 4718592 | tf_op jit(solution)/shard_map/prefix_grads/pallas_call | solution.py:318
  35.8 2.1 %place_tiles.1 = (bf16[24,64,512]{2,1,0:T(8,128)(2,1)}, bf16[1,128,128]{2,1,0:T(8,128)(2,1)}, bf16[1,128,128]{2,1,0:T(8,128)(2,1)}) custom-call(bf16[8,3,64,512]{3,2,1,0:T(8,128)(2,1)S(1)} %get-tuple-element.6.dq_ref, bf16[1,128,128]{2,1,0:T(8,128)(2,1)S(1)} %get-tuple-element.7.kg_ref, bf16[1,128,128]{2,1,0:T(8,128)(2,1)S(1)} %get-tuple-element.8.vg_ref, ...), custom_call_target="tpu_custom_call" | custom-call | tf_op jit(solution)/shard_map/place_tiles/pallas_call | solution.py:367

commit v4 on v3

--- a/solution.py
+++ b/solution.py
@@ -79,8 +79,11 @@
 
     loads[0].wait()
     loads[1].wait()
-    for d in range(1, line):
+    def send_along(d):
         kv_copy(dp, kv_line_send.at[d], peer(d)).start()
+
+    if line > 1:
+        send_along(1)
     kv_copy(dp, kv_par_send.at[0], partner()).start()
     kv_copy(dp, kv_sib_send.at[dp], sibling()).start()
 
@@ -113,6 +116,9 @@
                 )
             pieces.append(piece)
         flat[...] = jnp.concatenate(pieces, axis=1)
+
+    if line > 2:
+        send_along(2)
 
     def stacked(ref, t):
         tile = ref[t]
@@ -212,17 +218,21 @@
 
         @pl.when(s == 0)
         def _():
-            if line > 1:
-                forward_along(1)
+            for d in range(3, line):
+                send_along(d)
             forward_across(0)
 
-        @pl.when(odd & (half + 1 < line))
-        def _():
-            forward_along(half + 1)
-
-        @pl.when(odd & (half < line))
-        def _():
-            forward_across(half)
+        @pl.when(s + 1 < line)
+        def _():
+            forward_along(s + 1)
+
+        @pl.when((s == 1) & (line > 1))
+        def _():
+            forward_across(1)
+
+        @pl.when((lax.rem(s, 2) == 0) & (s >= 2) & (half + 1 < line))
+        def _():
+            forward_across(half + 1)
 
         @pl.when(odd & (s >= 3))
         def _():

time: 38 us -> 37.9 us (level)
  no operation moved by 1% of the time
where the time goes in v4:
time: 37.9 us; the launch traced here: 37.7 us
  Pallas kernels  37.1 us (98%)
  between operations  0.64 us (2%)
    pallas_call x1, Pallas kernels, shards(): pl.pallas_call(functools.partial(exchange_kernel, cap), out_shape=(jax.Sh...  35 us
    pallas_call x1, Pallas kernels, shards(): pl.pallas_call(functools.partial(place_kernel, cap), out_shape=(jax.Shape...  2.06 us

profile of v4, /device:TPU:0, one launch (start us, length us, event | category | flops | bytes accessed | tf_op | source)
XLA Modules:
  0.0 37.7 jit_solution(12946404333616012851)
XLA Ops:
  0.6 35.0 %prefix_grads.1 = (bf16[8,3,64,512]{3,2,1,0:T(8,128)(2,1)S(1)}, bf16[1,128,128]{2,1,0:T(8,128)(2,1)S(1)}, bf16[1,128,128]{2,1,0:T(8,128)(2,1)S(1)}) custom-call(bf16[24,64,512]{2,1,0:T(8,128)(2,1)} %q_hbm.1, bf16[24,64,512]{2,1,0:T(8,128)(2,1)} %g_hbm.1, bf16[1,128,128]{2,1,0:T(8,128)(2,1)} %k_hbm.1, bf16[1,128,128]{2,1,0:T(8,128)(2,1)} %v_hbm.1, ...), custom_call_target="tpu_custom_call" | custom-call | flops 2013265920 | bytes 4718592 | tf_op jit(solution)/shard_map/prefix_grads/pallas_call | solution.py:328
  35.7 2.1 %place_tiles.1 = (bf16[24,64,512]{2,1,0:T(8,128)(2,1)}, bf16[1,128,128]{2,1,0:T(8,128)(2,1)}, bf16[1,128,128]{2,1,0:T(8,128)(2,1)}) custom-call(bf16[8,3,64,512]{3,2,1,0:T(8,128)(2,1)S(1)} %get-tuple-element.6.dq_ref, bf16[1,128,128]{2,1,0:T(8,128)(2,1)S(1)} %get-tuple-element.7.kg_ref, bf16[1,128,128]{2,1,0:T(8,128)(2,1)S(1)} %get-tuple-element.8.vg_ref, ...), custom_call_target="tpu_custom_call" | custom-call | tf_op jit(solution)/shard_map/place_tiles/pallas_call | solution.py:377

commit v5 on v4

--- a/solution.py
+++ b/solution.py
@@ -17,6 +17,7 @@
     q_hbm, g_hbm, k_hbm, v_hbm, tp_hbm, lse_hbm, dot_hbm,
     dq_ref, kg_ref, vg_ref,
     tp_ref, q_ref, g_ref, kv, lse_raw, dot_raw, lse_rows, dot_rows, slots,
+    scores_ref, change_ref, probs_ref, score_grad_ref,
     part, sib_out, sib_in, par_out, par_in, line_out, line_in,
     in_sem, kv_recv, kv_sib_send, kv_par_send, kv_line_send,
     sib_send, sib_recv, par_send, par_recv, line_send, line_recv,
@@ -134,27 +135,33 @@
         found = [jnp.maximum(t, 0) for t in named]
         query = [stacked(q_ref, t) for t in found]
         grad = [stacked(g_ref, t) for t in found]
-        probs, score_grad = [], []
+        count = heads * rows
         for c in range(cap):
-            scores = lax.dot_general(keys, query[c], nt, preferred_element_type=f32)
-            prob_grad = lax.dot_general(values, grad[c], nt, preferred_element_type=f32)
-            suffix_l = lse_rows[pl.ds(found[c], 1), :] * LOG2E
+            here = slice(c * count, (c + 1) * count)
+            scores_ref[:, here] = lax.dot_general(keys, query[c], nt, preferred_element_type=f32)
+            change_ref[:, here] = lax.dot_general(values, grad[c], nt, preferred_element_type=f32)
+        for c in range(cap):
+            suffix_l = lse_rows[pl.ds(found[c], 1), :]
             suffix_d = dot_rows[pl.ds(found[c], 1), :]
-            scores = scores * (scaling * LOG2E)
-            top = jnp.maximum(jnp.max(scores, axis=0, keepdims=True), suffix_l)
-            shifted = jnp.exp2(scores - top)
-            suffix_w = jnp.exp2(suffix_l - top)
-            mass = jnp.sum(shifted, axis=0, keepdims=True) + suffix_w
-            moment = jnp.sum(shifted * prob_grad, axis=0, keepdims=True) + suffix_w * suffix_d
-            inverse = 1.0 / mass
-            delta = moment * inverse
-            if not full:
-                inverse = jnp.where(named[c] >= 0, inverse, 0.0)
-            weights = shifted * inverse
-            probs.append(weights.astype(jnp.bfloat16))
-            score_grad.append((weights * (prob_grad - delta)).astype(jnp.bfloat16))
-        probs = jnp.concatenate(probs, axis=1)
-        score_grad = jnp.concatenate(score_grad, axis=1)
+            for first in range(0, count, 128):
+                lanes = slice(first, first + 128)
+                here = slice(c * count + first, c * count + first + 128)
+                scores = scores_ref[:, here]
+                top = jnp.max(scores, axis=0, keepdims=True)
+                top = jnp.maximum(top, suffix_l[:, lanes] * (1.0 / scaling))
+                shifted = jnp.exp2((scores - top) * (scaling * LOG2E))
+                suffix_w = jnp.exp2((suffix_l[:, lanes] * (1.0 / scaling) - top) * (scaling * LOG2E))
+                mass = jnp.sum(shifted, axis=0, keepdims=True) + suffix_w
+                moment = jnp.sum(shifted * change_ref[:, here], axis=0, keepdims=True)
+                inverse = 1.0 / mass
+                delta = (moment + suffix_w * suffix_d[:, lanes]) * inverse
+                if not full:
+                    inverse = jnp.where(named[c] >= 0, inverse, 0.0)
+                weights = shifted * inverse
+                probs_ref[:, here] = weights.astype(jnp.bfloat16)
+                change = weights * (change_ref[:, here] - delta)
+                score_grad_ref[:, here] = change.astype(jnp.bfloat16)
+        probs, score_grad = probs_ref[...], score_grad_ref[...]
         value_sum = jnp.dot(probs, jnp.concatenate(grad, axis=0), preferred_element_type=f32)
         key_sum = jnp.dot(score_grad, jnp.concatenate(query, axis=0), preferred_element_type=f32)
         key_sum = key_sum * scaling
@@ -246,32 +253,33 @@
 
     lax.fori_loop(0, 2 * line, step, 0)
     to_partner(0)
+
+    for d in range(1, line):
+        kv_copy(dp, kv_line_send.at[d], peer(d)).wait_send()
+
+    def drain(d, carry):
+        kv_copy(along(d) * 2 + b, kv_par_send.at[d], partner()).wait_send()
+        return carry
+
+    def drain_prefix(p, carry):
+        kv_copy(p, kv_sib_send.at[p], sibling()).wait_send()
+        sib_copy(p).wait_send()
+        return carry
+
+    lax.fori_loop(0, line, drain, 0)
+    lax.fori_loop(0, prefixes, drain_prefix, 0)
     if line > 1:
         to_owner(line - 1)
+    for d in range(line):
+        par_copy(d).wait_send()
     total = chip_sum(0)
     for d in range(1, line):
         line_copy(d).wait_recv()
         total = total + line_in[d].astype(f32)
     kg_ref[0] = total[0].astype(jnp.bfloat16)
     vg_ref[0] = total[1].astype(jnp.bfloat16)
-
     for d in range(1, line):
-        kv_copy(dp, kv_line_send.at[d], peer(d)).wait_send()
         line_copy(d).wait_send()
-
-    def drain(d, carry):
-        kv_copy(along(d) * 2 + b, kv_par_send.at[d], partner()).wait_send()
-        par_copy(d).wait_send()
-        return carry
-
-    lax.fori_loop(0, line, drain, 0)
-
-    def drain_prefix(p, carry):
-        kv_copy(p, kv_sib_send.at[p], sibling()).wait_send()
-        sib_copy(p).wait_send()
-        return carry
-
-    lax.fori_loop(0, prefixes, drain_prefix, 0)
 
 
 def place_kernel(cap, dq_ref, kg_ref, vg_ref, tp_ref, out_hbm, kg_out, vg_out, counts, sem, small):
@@ -344,6 +352,10 @@
             pltpu.VMEM((tiles, heads * rows), f32),
             pltpu.VMEM((tiles, heads * rows), f32),
             pltpu.SMEM((prefixes * cap,), jnp.int32),
+            pltpu.VMEM((block * pos_count, cap * heads * rows), f32),
+            pltpu.VMEM((block * pos_count, cap * heads * rows), f32),
+            pltpu.VMEM((block * pos_count, cap * heads * rows), bf16),
+            pltpu.VMEM((block * pos_count, cap * heads * rows), bf16),
             pltpu.VMEM((prefixes,) + pair, f32),
             pltpu.VMEM((prefixes,) + pair, bf16),
             pltpu.VMEM((prefixes,) + pair, bf16),

time: 37.9 us -> 38.1 us (level)
  no operation moved by 1% of the time
where the time goes in v5:
time: 38.1 us; the launch traced here: 38 us
  Pallas kernels  37.3 us (98%)
  between operations  0.64 us (2%)
    pallas_call x1, Pallas kernels, shards(): pl.pallas_call(functools.partial(exchange_kernel, cap), out_shape=(jax.Sh...  35.3 us
    pallas_call x1, Pallas kernels, shards(): pl.pallas_call(functools.partial(place_kernel, cap), out_shape=(jax.Shape...  2.06 us

profile of v5, /device:TPU:0, one launch (start us, length us, event | category | flops | bytes accessed | tf_op | source)
XLA Modules:
  0.0 38.0 jit_solution(17115931554936999246)
XLA Ops:
  0.6 35.3 %prefix_grads.1 = (bf16[8,3,64,512]{3,2,1,0:T(8,128)(2,1)S(1)}, bf16[1,128,128]{2,1,0:T(8,128)(2,1)S(1)}, bf16[1,128,128]{2,1,0:T(8,128)(2,1)S(1)}) custom-call(bf16[24,64,512]{2,1,0:T(8,128)(2,1)} %q_hbm.1, bf16[24,64,512]{2,1,0:T(8,128)(2,1)} %g_hbm.1, bf16[1,128,128]{2,1,0:T(8,128)(2,1)} %k_hbm.1, bf16[1,128,128]{2,1,0:T(8,128)(2,1)} %v_hbm.1, ...), custom_call_target="tpu_custom_call" | custom-call | flops 2013265920 | bytes 4718592 | tf_op jit(solution)/shard_map/prefix_grads/pallas_call | solution.py:336
  35.9 2.1 %place_tiles.1 = (bf16[24,64,512]{2,1,0:T(8,128)(2,1)}, bf16[1,128,128]{2,1,0:T(8,128)(2,1)}, bf16[1,128,128]{2,1,0:T(8,128)(2,1)}) custom-call(bf16[8,3,64,512]{3,2,1,0:T(8,128)(2,1)S(1)} %get-tuple-element.6.dq_ref, bf16[1,128,128]{2,1,0:T(8,128)(2,1)S(1)} %get-tuple-element.7.kg_ref, bf16[1,128,128]{2,1,0:T(8,128)(2,1)S(1)} %get-tuple-element.8.vg_ref, ...), custom_call_target="tpu_custom_call" | custom-call | tf_op jit(solution)/shard_map/place_tiles/pallas_call | solution.py:389

commit v6 on v5

v6 whole, which is shorter than its diff:
```python
import functools
import math

import jax
import jax.numpy as jnp
from jax import lax
from jax.experimental import pallas as pl
from jax.experimental.pallas import tpu as pltpu
from jax.sharding import PartitionSpec as P

MESH = pl.DeviceIdType.MESH
LOG2E = 1.0 / math.log(2.0)


def neighbours(line):
    dp, pos = lax.axis_index("dp"), lax.axis_index("pos")
    a, b = dp // 2, lax.rem(dp, 2)
    sibling = {"pos": 1 - pos}
    partner = {"dp": a * 2 + 1 - b}

    def along(d):
        return lax.rem(a + d, line)

    def peer(d):
        return {"dp": along(d) * 2 + b}

    return dp, pos, b, sibling, partner, along, peer


def greet(line, sibling, partner, peer):
    barrier = pltpu.get_barrier_semaphore()
    pl.semaphore_signal(barrier, inc=1, device_id=sibling, device_id_type=MESH)
    pl.semaphore_signal(barrier, inc=1, device_id=partner, device_id_type=MESH)
    for d in range(1, line):
        pl.semaphore_signal(barrier, inc=1, device_id=peer(d), device_id_type=MESH)
    pl.semaphore_wait(barrier, line + 1)


def remote(src, dst, send, recv, device):
    return pltpu.make_async_remote_copy(
        src_ref=src, dst_ref=dst, send_sem=send, recv_sem=recv,
        device_id=device, device_id_type=MESH,
    )


def gather_kernel(k_hbm, v_hbm, out_ref, kv, in_sem, kv_recv, kv_sib_send, kv_par_send, kv_line_send):
    prefixes = kv.shape[0]
    line = prefixes // 2
    dp, pos, b, sibling, partner, along, peer = neighbours(line)
    loads = [
        pltpu.make_async_copy(k_hbm.at[0], kv.at[dp, pos, 0], in_sem.at[0]),
        pltpu.make_async_copy(v_hbm.at[0], kv.at[dp, pos, 1], in_sem.at[1]),
    ]
    for load in loads:
        load.start()
    greet(line, sibling, partner, peer)
    for load in loads:
        load.wait()

    def kv_copy(p, send, device):
        mine = kv.at[p, pos]
        return remote(mine, mine, send, kv_recv.at[p, pos], device)

    def kv_wait(p, which):
        here = kv.at[p, which]
        remote(here, here, kv_sib_send.at[p], kv_recv.at[p, which], sibling).wait_recv()

    for d in range(1, line):
        kv_copy(dp, kv_line_send.at[d], peer(d)).start()
    kv_copy(dp, kv_par_send.at[0], partner).start()
    kv_copy(dp, kv_sib_send.at[dp], sibling).start()

    def forward_along(d, carry):
        p = along(d) * 2 + b
        kv_wait(p, pos)
        kv_copy(p, kv_par_send.at[d], partner).start()
        kv_copy(p, kv_sib_send.at[p], sibling).start()
        return carry

    def forward_across(d, carry):
        p = along(d) * 2 + 1 - b
        kv_wait(p, pos)
        kv_copy(p, kv_sib_send.at[p], sibling).start()
        return carry

    lax.fori_loop(1, line, forward_along, 0)
    lax.fori_loop(0, line, forward_across, 0)

    def receive(p, carry):
        kv_wait(p, 1 - pos)
        return carry

    def drain(p, carry):
        kv_copy(p, kv_sib_send.at[p], sibling).wait_send()
        return carry

    lax.fori_loop(0, prefixes, receive, 0)
    lax.fori_loop(0, prefixes, drain, 0)
    for d in range(line):
        kv_copy(along(d) * 2 + b, kv_par_send.at[d], partner).wait_send()
    for d in range(1, line):
        kv_copy(dp, kv_line_send.at[d], peer(d)).wait_send()
    out_ref[...] = kv[...]


def product_kernel(
    cap,
    q_hbm, g_hbm, kv, tp_hbm, lse_hbm, dot_hbm,
    dq_hbm, part, sib_out,
    tp_ref, q_ref, g_ref, dq_ref, lse_raw, dot_raw, lse_rows, dot_rows, slots,
    scores_ref, change_ref, probs_ref, score_grad_ref,
    in_sem, dq_sem,
):
    tiles, rows, width = q_ref.shape
    prefixes, pos_count, _, block, dim = kv.shape
    heads = width // dim
    dp, pos = lax.axis_index("dp"), lax.axis_index("pos")
    scaling = dim ** (-0.5)
    full = cap * prefixes == tiles
    base = dp * tiles
    loads = [
        pltpu.make_async_copy(lse_hbm.at[pl.ds(base, tiles)], lse_raw, in_sem.at[0]),
        pltpu.make_async_copy(dot_hbm.at[pl.ds(base, tiles)], dot_raw, in_sem.at[1]),
        pltpu.make_async_copy(q_hbm, q_ref, in_sem.at[2]),
        pltpu.make_async_copy(g_hbm, g_ref, in_sem.at[3]),
    ]
    named_load = pltpu.make_async_copy(tp_hbm, tp_ref, in_sem.at[4])
    named_load.start()
    for load in loads:
        load.start()

    def out_copy(p, c, t):
        return pltpu.make_async_copy(dq_ref.at[p, c], dq_hbm.at[t], dq_sem.at[p, c])

    named_load.wait()

    def find(p, carry):
        def look(i, found):
            t = tiles - 1 - i
            hit = tp_ref[0, base + t] == p
            shifted = (t,) + found[:-1]
            return tuple(jnp.where(hit, new, old) for new, old in zip(shifted, found))

        found = lax.fori_loop(0, tiles, look, (jnp.int32(-1),) * cap, unroll=True)
        for c in range(cap):
            slots[p * cap + c] = found[c]
        return carry

    lax.fori_loop(0, prefixes, find, 0)

    for load in loads:
        load.wait()
    for raw, flat in ((lse_raw, lse_rows), (dot_raw, dot_rows)):
        pieces = []
        for h in range(heads):
            row = raw[:, h, :]
            piece = row[:, :rows]
            for other_pos in range(1, pos_count):
                piece = jnp.where(
                    pos == other_pos, row[:, other_pos * rows:(other_pos + 1) * rows], piece
                )
            pieces.append(piece)
        flat[...] = jnp.concatenate(pieces, axis=1)


    def stacked(ref, t):
        tile = ref[t]
        return jnp.concatenate([tile[:, h * dim:(h + 1) * dim] for h in range(heads)], axis=0)

    nt = (((1,), (1,)), ((), ()))
    f32 = jnp.float32

    def compute(p, carry):
        keys = jnp.concatenate([kv[p, i, 0] for i in range(pos_count)], axis=0)
        values = jnp.concatenate([kv[p, i, 1] for i in range(pos_count)], axis=0)
        named = [slots[p * cap + c] for c in range(cap)]
        found = [jnp.maximum(t, 0) for t in named]
        query = [stacked(q_ref, t) for t in found]
        grad = [stacked(g_ref, t) for t in found]
        count = heads * rows
        for c in range(cap):
            here = slice(c * count, (c + 1) * count)
            scores_ref[:, here] = lax.dot_general(keys, query[c], nt, preferred_element_type=f32)
            change_ref[:, here] = lax.dot_general(values, grad[c], nt, preferred_element_type=f32)
        for c in range(cap):
            suffix_l = lse_rows[pl.ds(found[c], 1), :]
            suffix_d = dot_rows[pl.ds(found[c], 1), :]
            for first in range(0, count, 128):
                lanes = slice(first, first + 128)
                here = slice(c * count + first, c * count + first + 128)
                scores = scores_ref[:, here]
                top = jnp.max(scores, axis=0, keepdims=True)
                top = jnp.maximum(top, suffix_l[:, lanes] * (1.0 / scaling))
                shifted = jnp.exp2((scores - top) * (scaling * LOG2E))
                suffix_w = jnp.exp2((suffix_l[:, lanes] * (1.0 / scaling) - top) * (scaling * LOG2E))
                mass = jnp.sum(shifted, axis=0, keepdims=True) + suffix_w
                moment = jnp.sum(shifted * change_ref[:, here], axis=0, keepdims=True)
                inverse = 1.0 / mass
                delta = (moment + suffix_w * suffix_d[:, lanes]) * inverse
                if not full:
                    inverse = jnp.where(named[c] >= 0, inverse, 0.0)
                weights = shifted * inverse
                probs_ref[:, here] = weights.astype(jnp.bfloat16)
                change = weights * (change_ref[:, here] - delta)
                score_grad_ref[:, here] = change.astype(jnp.bfloat16)
        probs, score_grad = probs_ref[...], score_grad_ref[...]
        value_sum = jnp.dot(probs, jnp.concatenate(grad, axis=0), preferred_element_type=f32)
        key_sum = jnp.dot(score_grad, jnp.concatenate(query, axis=0), preferred_element_type=f32)
        key_sum = key_sum * scaling
        for i, total in enumerate((key_sum, value_sum)):
            low, high = total[:block], total[block:]
            part[p, i] = jnp.where(pos == 0, low, high)
            sib_out[p, i] = jnp.where(pos == 0, high, low).astype(jnp.bfloat16)
        query_part = jnp.dot(keys.T, score_grad, preferred_element_type=f32)
        query_part = (query_part * scaling).astype(jnp.bfloat16).T
        for c in range(cap):
            for h in range(heads):
                first = (c * heads + h) * rows
                dq_ref[p, c, :, h * dim:(h + 1) * dim] = query_part[first:first + rows]

            @pl.when(named[c] >= 0)
            def _():
                out_copy(p, c, found[c]).start()

        return carry

    lax.fori_loop(0, prefixes, compute, 0)

    def finish(p, carry):
        for c in range(cap):
            t = slots[p * cap + c]

            @pl.when(t >= 0)
            def _():
                out_copy(p, c, jnp.maximum(t, 0)).wait()

        return carry

    lax.fori_loop(0, prefixes, finish, 0)


def reduce_kernel(
    part, sib_first, kg_ref, vg_ref,
    sib_out, sib_in, par_out, par_in, line_out, line_in,
    sib_send, sib_recv, par_send, par_recv, line_send, line_recv,
):
    prefixes = part.shape[0]
    line = prefixes // 2
    f32 = jnp.float32
    dp, pos, b, sibling, partner, along, peer = neighbours(line)
    sib_out[...] = sib_first[...]
    greet(line, sibling, partner, peer)

    def sib_copy(p):
        return remote(sib_out.at[p], sib_in.at[p], sib_send.at[p], sib_recv.at[p], sibling)

    def par_copy(d):
        return remote(par_out.at[d], par_in.at[d], par_send.at[d], par_recv.at[d], partner)

    def line_copy(d):
        return remote(line_out.at[d], line_in.at[d], line_send.at[d], line_recv.at[d], peer(d))

    def to_partner(d):
        p = along(d) * 2 + 1 - b
        sib_copy(p).wait_recv()
        par_out[d] = (part[p] + sib_in[p].astype(f32)).astype(jnp.bfloat16)
        par_copy(d).start()

    def chip_sum(d):
        p = along(d) * 2 + b
        sib_copy(p).wait_recv()
        par_copy(d).wait_recv()
        return part[p] + sib_in[p].astype(f32) + par_in[d].astype(f32)

    order = [d % line for d in range(1, line + 1)]
    for d in order:
        sib_copy(along(d) * 2 + 1 - b).start()
    for d in order:
        sib_copy(along(d) * 2 + b).start()
    for d in order:
        to_partner(d)
    for d in range(1, line):
        line_out[d] = chip_sum(d).astype(jnp.bfloat16)
        line_copy(d).start()
    for p in range(prefixes):
        sib_copy(p).wait_send()
    for d in range(line):
        par_copy(d).wait_send()
    total = chip_sum(0)
    for d in range(1, line):
        line_copy(d).wait_recv()
        total = total + line_in[d].astype(f32)
    kg_ref[0] = total[0].astype(jnp.bfloat16)
    vg_ref[0] = total[1].astype(jnp.bfloat16)
    for d in range(1, line):
        line_copy(d).wait_send()


def stay(array):
    return pltpu.with_memory_space_constraint(array, pltpu.HBM)


def shards(
    queries, output_gradient, prefix_keys, prefix_values, tile_prefix, suffix_lse, suffix_dot
):
    prefixes = lax.axis_size("dp")
    pos_count = lax.axis_size("pos")
    tiles, rows, width = queries.shape
    _, block, dim = prefix_keys.shape
    heads = width // dim
    tile_rows = rows * pos_count
    cap = max(2, tiles // prefixes)
    line = prefixes // 2
    bf16, f32 = jnp.bfloat16, jnp.float32
    hbm_spec = pl.BlockSpec(memory_space=pltpu.HBM)
    vmem_spec = pl.BlockSpec(memory_space=pltpu.VMEM)
    dma = pltpu.SemaphoreType.DMA
    pair = (2, block, dim)
    kv = pl.pallas_call(
        gather_kernel,
        out_shape=jax.ShapeDtypeStruct((prefixes, pos_count) + pair, bf16),
        in_specs=[hbm_spec] * 2,
        out_specs=vmem_spec,
        scratch_shapes=[
            pltpu.VMEM((prefixes, pos_count) + pair, bf16),
            dma((2,)),
            dma((prefixes, pos_count)),
            dma((prefixes,)),
            dma((line,)),
            dma((line,)),
        ],
        compiler_params=pltpu.CompilerParams(
            collective_id=0, has_side_effects=True, vmem_limit_bytes=24 << 20
        ),
        name="gather_prefixes",
    )(stay(prefix_keys), stay(prefix_values))
    wide = (block * pos_count, cap * heads * rows)
    query_grad, part, sib_out = pl.pallas_call(
        functools.partial(product_kernel, cap),
        out_shape=(
            jax.ShapeDtypeStruct(queries.shape, bf16),
            jax.ShapeDtypeStruct((prefixes,) + pair, f32),
            jax.ShapeDtypeStruct((prefixes,) + pair, bf16),
        ),
        in_specs=[hbm_spec] * 2 + [vmem_spec] + [hbm_spec] * 3,
        out_specs=(hbm_spec, vmem_spec, vmem_spec),
        scratch_shapes=[
            pltpu.SMEM(tile_prefix.shape[::-1], jnp.int32),
            pltpu.VMEM((tiles, rows, width), bf16),
            pltpu.VMEM((tiles, rows, width), bf16),
            pltpu.VMEM((prefixes, cap, rows, width), bf16),
            pltpu.VMEM((tiles, heads, tile_rows), f32),
            pltpu.VMEM((tiles, heads, tile_rows), f32),
            pltpu.VMEM((tiles, heads * rows), f32),
            pltpu.VMEM((tiles, heads * rows), f32),
            pltpu.SMEM((prefixes * cap,), jnp.int32),
            pltpu.VMEM(wide, f32),
            pltpu.VMEM(wide, f32),
            pltpu.VMEM(wide, bf16),
            pltpu.VMEM(wide, bf16),
            dma((5,)),
            dma((prefixes, cap)),
        ],
        compiler_params=pltpu.CompilerParams(vmem_limit_bytes=24 << 20),
        name="tile_products",
    )(
        stay(queries), stay(output_gradient), kv, stay(tile_prefix.T),
        stay(jnp.swapaxes(suffix_lse, 1, 2)), stay(jnp.swapaxes(suffix_dot, 1, 2)),
    )
    key_grad, value_grad = pl.pallas_call(
        reduce_kernel,
        out_shape=(
            jax.ShapeDtypeStruct(prefix_keys.shape, bf16),
            jax.ShapeDtypeStruct(prefix_values.shape, bf16),
        ),
        in_specs=[vmem_spec] * 2,
        out_specs=(vmem_spec, vmem_spec),
        scratch_shapes=[
            pltpu.VMEM((prefixes,) + pair, bf16),
            pltpu.VMEM((prefixes,) + pair, bf16),
            pltpu.VMEM((line,) + pair, bf16),
            pltpu.VMEM((line,) + pair, bf16),
            pltpu.VMEM((line,) + pair, bf16),
            pltpu.VMEM((line,) + pair, bf16),
        ] + [dma((prefixes,))] * 2 + [dma((line,))] * 4,
        compiler_params=pltpu.CompilerParams(
            collective_id=1, has_side_effects=True, vmem_limit_bytes=24 << 20
        ),
        name="reduce_grads",
    )(part, sib_out)
    return query_grad, key_grad, value_grad


def solution(mesh):
    in_specs = (
        P("dp", "pos", "head"),
        P("dp", "pos", "head"),
        P("dp", "pos", "head"),
        P("dp", "pos", "head"),
        P(),
        P(None, None, "head"),
        P(None, None, "head"),
    )
    out_specs = (P("dp", "pos", "head"), P("dp", "pos", "head"), P("dp", "pos", "head"))
    return jax.shard_map(shards, mesh=mesh, in_specs=in_specs, out_specs=out_specs, check_vma=False)
```

time: 38.1 us -> 45.2 us (1.19)
  Pallas kernels: 37.3 us -> 43.1 us
  local copies, waits for them, and re-layouts: 0 us -> 1.23 us
    pallas_call x2 -> x3, Pallas kernels: 37.3 us -> 43.1 us  [the longest x1 17.7 us: shards(): pl.pallas_call(gather_kernel, out_shape=jax.ShapeDtypeStruct((prefixes, p...]
    unnamed x0 -> x2, local copies, waits for them, and re-layouts: none -> 1.23 us
where the time goes in v6:
time: 45.2 us; the launch traced here: 45 us
  Pallas kernels  43.1 us (95%)
  local copies, waits for them, and re-layouts  1.23 us (3%)
  between operations  0.65 us (1%)
    pallas_call x1, Pallas kernels, shards(): pl.pallas_call(gather_kernel, out_shape=jax.ShapeDtypeStruct((prefixes, p...  17.7 us
    pallas_call x1, Pallas kernels, shards(): pl.pallas_call(reduce_kernel, out_shape=(jax.ShapeDtypeStruct(prefix_keys...  13.9 us
    pallas_call x1, Pallas kernels, shards(): pl.pallas_call(functools.partial(product_kernel, cap), out_shape=(jax.Sha...  11.5 us
    unnamed x2, local copies, waits for them, and re-layouts  1.23 us

profile of v6, /device:TPU:0, one launch (start us, length us, event | category | flops | bytes accessed | tf_op | source)
XLA Modules:
  0.0 45.0 jit_solution(3126520390262243734)
XLA Ops:
  0.6 17.7 %gather_prefixes.1.kv = bf16[8,2,2,128,128]{4,3,2,1,0:T(8,128)(2,1)S(1)} custom-call(bf16[1,128,128]{2,1,0:T(8,128)(2,1)} %k_hbm.1, bf16[1,128,128]{2,1,0:T(8,128)(2,1)} %v_hbm.1), custom_call_target="tpu_custom_call" | custom-call | tf_op jit(solution)/shard_map/gather_prefixes/pallas_call | solution.py:319
  18.3 11.5 %tile_products.1 = (bf16[24,64,512]{2,1,0:T(8,128)(2,1)}, f32[8,2,128,128]{3,2,1,0:T(8,128)S(1)}, bf16[8,2,128,128]{3,2,1,0:T(8,128)(2,1)S(1)}) custom-call(bf16[24,64,512]{2,1,0:T(8,128)(2,1)} %q_hbm.1, bf16[24,64,512]{2,1,0:T(8,128)(2,1)} %g_hbm.1, bf16[8,2,2,128,128]{4,3,2,1,0:T(8,128)(2,1)S(1)} %gather_prefixes.1.kv, s32[1,192]{1,0:T(1,128)} %bitcast.5, ...), custom_call_target="tpu_custom_call" | custom-call | tf_op jit(solution)/shard_map/tile_products/pallas_call | solution.py:338
  29.9 13.9 %reduce_grads.1 = (bf16[1,128,128]{2,1,0:T(8,128)(2,1)S(1)}, bf16[1,128,128]{2,1,0:T(8,128)(2,1)S(1)}) custom-call(f32[8,2,128,128]{3,2,1,0:T(8,128)S(1)} %get-tuple-element.9.part, bf16[8,2,128,128]{3,2,1,0:T(8,128)(2,1)S(1)} %get-tuple-element.10.sib_first), custom_call_target="tpu_custom_call" | custom-call | tf_op jit(solution)/shard_map/reduce_grads/pallas_call | solution.py:370
  43.8 0.6 %copy.12 = bf16[1,128,128]{2,1,0:T(8,128)(2,1)} copy(bf16[1,128,128]{2,1,0:T(8,128)(2,1)S(1)} %get-tuple-element.17) | data formatting | bytes 65536
  44.4 0.6 %copy.13 = bf16[1,128,128]{2,1,0:T(8,128)(2,1)} copy(bf16[1,128,128]{2,1,0:T(8,128)(2,1)S(1)} %get-tuple-element.18) | data formatting | bytes 65536

commit v7 on v5

--- a/solution.py
+++ b/solution.py
@@ -215,11 +215,13 @@
         kv_wait(p, pos)
         kv_copy(p, kv_sib_send.at[p], sibling()).start()
 
+    last = 2 * line - 2 if line > 1 else 2
+
     def step(s, carry):
-        half = (s + 1) // 2
+        half = s // 2
         odd = lax.rem(s, 2) == 1
-        across = ((s > 0) & (lax.rem(s, 2) == 0)) | (s == 2 * line - 1)
-        p = along(lax.rem(half, line)) * 2 + jnp.where(across, other, b)
+        across = (odd & (s < last)) | (s == last)
+        p = along(half) * 2 + jnp.where(across, other, b)
         kv_wait(p, 1 - pos)
         compute(p)
 
@@ -233,26 +235,28 @@
         def _():
             forward_along(s + 1)
 
-        @pl.when((s == 1) & (line > 1))
-        def _():
-            forward_across(1)
-
-        @pl.when((lax.rem(s, 2) == 0) & (s >= 2) & (half + 1 < line))
+        @pl.when(odd & (s <= 3) & (half + 1 < line))
         def _():
             forward_across(half + 1)
 
-        @pl.when(odd & (s >= 3))
+        @pl.when((lax.rem(s, 2) == 0) & (s >= 4) & (half + 1 < line))
+        def _():
+            forward_across(half + 1)
+
+        @pl.when((lax.rem(s, 2) == 0) & (s >= 2))
         def _():
             to_partner(half - 1)
 
-        @pl.when((lax.rem(s, 2) == 0) & (s >= 4))
-        def _():
-            to_owner(half - 1)
+        @pl.when((lax.rem(s, 2) == 0) & (s >= 6))
+        def _():
+            to_owner(half - 2)
 
         return carry
 
     lax.fori_loop(0, 2 * line, step, 0)
-    to_partner(0)
+    to_partner(line - 1)
+    if line > 2:
+        to_owner(line - 2)
 
     for d in range(1, line):
         kv_copy(dp, kv_line_send.at[d], peer(d)).wait_send()

time: 38.1 us -> 34.7 us (0.911)
  Pallas kernels: 37.3 us -> 33.9 us
    pallas_call x1, Pallas kernels: 35.3 us -> 31.8 us  [shards(): pl.pallas_call(functools.partial(exchange_kernel, cap), out_shape=(jax.Sh...]
where the time goes in v7:
time: 34.7 us; the launch traced here: 34.5 us
  Pallas kernels  33.9 us (98%)
  between operations  0.64 us (2%)
    pallas_call x1, Pallas kernels, shards(): pl.pallas_call(functools.partial(exchange_kernel, cap), out_shape=(jax.Sh...  31.8 us
    pallas_call x1, Pallas kernels, shards(): pl.pallas_call(functools.partial(place_kernel, cap), out_shape=(jax.Shape...  2.06 us

profile of v7, /device:TPU:0, one launch (start us, length us, event | category | flops | bytes accessed | tf_op | source)
XLA Modules:
  0.0 34.5 jit_solution(13776044360931392333)
XLA Ops:
  0.6 31.8 %prefix_grads.1 = (bf16[8,3,64,512]{3,2,1,0:T(8,128)(2,1)S(1)}, bf16[1,128,128]{2,1,0:T(8,128)(2,1)S(1)}, bf16[1,128,128]{2,1,0:T(8,128)(2,1)S(1)}) custom-call(bf16[24,64,512]{2,1,0:T(8,128)(2,1)} %q_hbm.1, bf16[24,64,512]{2,1,0:T(8,128)(2,1)} %g_hbm.1, bf16[1,128,128]{2,1,0:T(8,128)(2,1)} %k_hbm.1, bf16[1,128,128]{2,1,0:T(8,128)(2,1)} %v_hbm.1, ...), custom_call_target="tpu_custom_call" | custom-call | flops 2013265920 | bytes 4718592 | tf_op jit(solution)/shard_map/prefix_grads/pallas_call | solution.py:340
  32.5 2.1 %place_tiles.1 = (bf16[24,64,512]{2,1,0:T(8,128)(2,1)}, bf16[1,128,128]{2,1,0:T(8,128)(2,1)}, bf16[1,128,128]{2,1,0:T(8,128)(2,1)}) custom-call(bf16[8,3,64,512]{3,2,1,0:T(8,128)(2,1)S(1)} %get-tuple-element.6.dq_ref, bf16[1,128,128]{2,1,0:T(8,128)(2,1)S(1)} %get-tuple-element.7.kg_ref, bf16[1,128,128]{2,1,0:T(8,128)(2,1)S(1)} %get-tuple-element.8.vg_ref, ...), custom_call_target="tpu_custom_call" | custom-call | tf_op jit(solution)/shard_map/place_tiles/pallas_call | solution.py:393

commit v8 on v7

--- a/solution.py
+++ b/solution.py
@@ -39,7 +39,8 @@
         return {"dp": a * 2 + other}
 
     def along(d):
-        return lax.rem(a + d, line)
+        offset = jnp.where(lax.rem(d, 2) == 1, (d + 1) // 2, line - d // 2)
+        return lax.rem(a + offset, line)
 
     def peer(d):
         return {"dp": along(d) * 2 + b}
@@ -83,8 +84,8 @@
     def send_along(d):
         kv_copy(dp, kv_line_send.at[d], peer(d)).start()
 
-    if line > 1:
-        send_along(1)
+    for d in range(1, min(line, 3)):
+        send_along(d)
     kv_copy(dp, kv_par_send.at[0], partner()).start()
     kv_copy(dp, kv_sib_send.at[dp], sibling()).start()
 
@@ -117,9 +118,6 @@
                 )
             pieces.append(piece)
         flat[...] = jnp.concatenate(pieces, axis=1)
-
-    if line > 2:
-        send_along(2)
 
     def stacked(ref, t):
         tile = ref[t]

time: 34.7 us -> 32.6 us (0.939)
  Pallas kernels: 33.9 us -> 31.8 us
    pallas_call x1, Pallas kernels: 31.8 us -> 29.8 us  [shards(): pl.pallas_call(functools.partial(exchange_kernel, cap), out_shape=(jax.Sh...]
where the time goes in v8:
time: 32.6 us; the launch traced here: 32.5 us
  Pallas kernels  31.8 us (98%)
  between operations  0.64 us (2%)
    pallas_call x1, Pallas kernels, shards(): pl.pallas_call(functools.partial(exchange_kernel, cap), out_shape=(jax.Sh...  29.8 us
    pallas_call x1, Pallas kernels, shards(): pl.pallas_call(functools.partial(place_kernel, cap), out_shape=(jax.Shape...  2.06 us

profile of v8, /device:TPU:0, one launch (start us, length us, event | category | flops | bytes accessed | tf_op | source)
XLA Modules:
  0.0 32.5 jit_solution(15460753821941359521)
XLA Ops:
  0.6 29.8 %prefix_grads.1 = (bf16[8,3,64,512]{3,2,1,0:T(8,128)(2,1)S(1)}, bf16[1,128,128]{2,1,0:T(8,128)(2,1)S(1)}, bf16[1,128,128]{2,1,0:T(8,128)(2,1)S(1)}) custom-call(bf16[24,64,512]{2,1,0:T(8,128)(2,1)} %q_hbm.1, bf16[24,64,512]{2,1,0:T(8,128)(2,1)} %g_hbm.1, bf16[1,128,128]{2,1,0:T(8,128)(2,1)} %k_hbm.1, bf16[1,128,128]{2,1,0:T(8,128)(2,1)} %v_hbm.1, ...), custom_call_target="tpu_custom_call" | custom-call | flops 2013265920 | bytes 4718592 | tf_op jit(solution)/shard_map/prefix_grads/pallas_call | solution.py:338
  30.4 2.1 %place_tiles.1 = (bf16[24,64,512]{2,1,0:T(8,128)(2,1)}, bf16[1,128,128]{2,1,0:T(8,128)(2,1)}, bf16[1,128,128]{2,1,0:T(8,128)(2,1)}) custom-call(bf16[8,3,64,512]{3,2,1,0:T(8,128)(2,1)S(1)} %get-tuple-element.6.dq_ref, bf16[1,128,128]{2,1,0:T(8,128)(2,1)S(1)} %get-tuple-element.7.kg_ref, bf16[1,128,128]{2,1,0:T(8,128)(2,1)S(1)} %get-tuple-element.8.vg_ref, ...), custom_call_target="tpu_custom_call" | custom-call | tf_op jit(solution)/shard_map/place_tiles/pallas_call | solution.py:391

commit v9 on v8

--- a/solution.py
+++ b/solution.py
@@ -15,8 +15,8 @@
 def exchange_kernel(
     cap,
     q_hbm, g_hbm, k_hbm, v_hbm, tp_hbm, lse_hbm, dot_hbm,
-    dq_ref, kg_ref, vg_ref,
-    tp_ref, q_ref, g_ref, kv, lse_raw, dot_raw, lse_rows, dot_rows, slots,
+    out_ref, kg_ref, vg_ref,
+    dq_ref, tp_ref, q_ref, g_ref, kv, lse_raw, dot_raw, lse_rows, dot_rows, slots,
     scores_ref, change_ref, probs_ref, score_grad_ref,
     part, sib_out, sib_in, par_out, par_in, line_out, line_in,
     in_sem, kv_recv, kv_sib_send, kv_par_send, kv_line_send,
@@ -256,11 +256,20 @@
     if line > 2:
         to_owner(line - 2)
 
-    for d in range(1, line):
-        kv_copy(dp, kv_line_send.at[d], peer(d)).wait_send()
+    if line > 1:
+        to_owner(line - 1)
+
+    def place(t, carry):
+        p = tp_ref[0, base + t]
+        c = jnp.int32(0)
+        for later in range(1, cap):
+            c = c + jnp.where(slots[p * cap + later] == t, later, 0)
+        out_ref[t] = dq_ref[p, c]
+        return carry
 
     def drain(d, carry):
         kv_copy(along(d) * 2 + b, kv_par_send.at[d], partner()).wait_send()
+        par_copy(d).wait_send()
         return carry
 
     def drain_prefix(p, carry):
@@ -268,12 +277,11 @@
         sib_copy(p).wait_send()
         return carry
 
+    lax.fori_loop(0, tiles, place, 0)
+    for d in range(1, line):
+        kv_copy(dp, kv_line_send.at[d], peer(d)).wait_send()
     lax.fori_loop(0, line, drain, 0)
     lax.fori_loop(0, prefixes, drain_prefix, 0)
-    if line > 1:
-        to_owner(line - 1)
-    for d in range(line):
-        par_copy(d).wait_send()
     total = chip_sum(0)
     for d in range(1, line):
         line_copy(d).wait_recv()
@@ -284,32 +292,20 @@
         line_copy(d).wait_send()
 
 
-def place_kernel(cap, dq_ref, kg_ref, vg_ref, tp_ref, out_hbm, kg_out, vg_out, counts, sem, small):
-    tiles = out_hbm.shape[0]
-    prefixes = dq_ref.shape[0]
-    base = lax.axis_index("dp") * tiles
-    kg_copy = pltpu.make_async_copy(kg_ref, kg_out, small.at[0])
-    vg_copy = pltpu.make_async_copy(vg_ref, vg_out, small.at[1])
-    kg_copy.start()
-    vg_copy.start()
-    for p in range(prefixes):
-        counts[p] = 0
-
-    def place(t, carry):
-        p = tp_ref[0, base + t]
-        c = counts[p]
-        counts[p] = c + 1
-        pltpu.make_async_copy(dq_ref.at[p, c], out_hbm.at[t], sem.at[t]).start()
-        return carry
-
-    def finish(t, carry):
-        pltpu.make_async_copy(dq_ref.at[0, 0], out_hbm.at[t], sem.at[t]).wait()
-        return carry
-
-    lax.fori_loop(0, tiles, place, 0)
-    lax.fori_loop(0, tiles, finish, 0)
-    kg_copy.wait()
-    vg_copy.wait()
+def write_kernel(dq_ref, kg_ref, vg_ref, dq_hbm, kg_hbm, vg_hbm, sem):
+    pieces = sem.shape[0] - 2
+    tiles = dq_ref.shape[0] // pieces
+    copies = [
+        pltpu.make_async_copy(kg_ref, kg_hbm, sem.at[pieces]),
+        pltpu.make_async_copy(vg_ref, vg_hbm, sem.at[pieces + 1]),
+    ]
+    for i in range(pieces):
+        here = pl.ds(i * tiles, tiles)
+        copies.append(pltpu.make_async_copy(dq_ref.at[here], dq_hbm.at[here], sem.at[i]))
+    for copy in copies:
+        copy.start()
+    for copy in copies:
+        copy.wait()
 
 
 def stay(array):
@@ -330,7 +326,6 @@
     bf16, f32 = jnp.bfloat16, jnp.float32
     named = stay(tile_prefix.T)
     hbm_spec = pl.BlockSpec(memory_space=pltpu.HBM)
-    smem_spec = pl.BlockSpec(memory_space=pltpu.SMEM)
     vmem_spec = pl.BlockSpec(memory_space=pltpu.VMEM)
     dma = pltpu.SemaphoreType.DMA
     pair = (2, block, dim)
@@ -338,13 +333,14 @@
     dq, kg, vg = pl.pallas_call(
         functools.partial(exchange_kernel, cap),
         out_shape=(
-            jax.ShapeDtypeStruct((prefixes, cap, rows, width), bf16),
+            jax.ShapeDtypeStruct(queries.shape, bf16),
             jax.ShapeDtypeStruct(prefix_keys.shape, bf16),
             jax.ShapeDtypeStruct(prefix_values.shape, bf16),
         ),
         in_specs=[hbm_spec] * 7,
         out_specs=(vmem_spec, vmem_spec, vmem_spec),
         scratch_shapes=[
+            pltpu.VMEM((prefixes, cap, rows, width), bf16),
             pltpu.SMEM(named.shape, jnp.int32),
             pltpu.VMEM((tiles, rows, width), bf16),
             pltpu.VMEM((tiles, rows, width), bf16),
@@ -389,18 +385,18 @@
         stay(jnp.swapaxes(suffix_lse, 1, 2)), stay(jnp.swapaxes(suffix_dot, 1, 2)),
     )
     return pl.pallas_call(
-        functools.partial(place_kernel, cap),
+        write_kernel,
         out_shape=(
             jax.ShapeDtypeStruct(queries.shape, bf16),
             jax.ShapeDtypeStruct(prefix_keys.shape, bf16),
             jax.ShapeDtypeStruct(prefix_values.shape, bf16),
         ),
-        in_specs=[vmem_spec] * 3 + [smem_spec],
+        in_specs=[vmem_spec] * 3,
         out_specs=(hbm_spec,) * 3,
-        scratch_shapes=[pltpu.SMEM((prefixes,), jnp.int32), dma((tiles,)), dma((2,))],
+        scratch_shapes=[dma((math.gcd(tiles, 8) + 2,))],
         compiler_params=pltpu.CompilerParams(vmem_limit_bytes=16 << 20),
-        name="place_tiles",
-    )(dq, kg, vg, named)
+        name="write_results",
+    )(dq, kg, vg)
 
 
 def solution(mesh):

time: 32.6 us -> 31.8 us (0.975)
  Pallas kernels: 31.8 us -> 31 us
    pallas_call x1, Pallas kernels: 2.06 us -> 1.24 us  [shards(): pl.pallas_call(write_kernel, out_shape=(jax.ShapeDtypeStruct(queries.shap...]
where the time goes in v9:
time: 31.8 us; the launch traced here: 31.6 us
  Pallas kernels  31 us (97%)
  between operations  0.64 us (2%)
    pallas_call x1, Pallas kernels, shards(): pl.pallas_call(functools.partial(exchange_kernel, cap), out_shape=(jax.Sh...  29.8 us
    pallas_call x1, Pallas kernels, shards(): pl.pallas_call(write_kernel, out_shape=(jax.ShapeDtypeStruct(queries.shap...  1.24 us

profile of v9, /device:TPU:0, one launch (start us, length us, event | category | flops | bytes accessed | tf_op | source)
XLA Modules:
  0.0 31.6 jit_solution(12558583205683055388)
XLA Ops:
  0.6 29.8 %prefix_grads.1 = (bf16[24,64,512]{2,1,0:T(8,128)(2,1)S(1)}, bf16[1,128,128]{2,1,0:T(8,128)(2,1)S(1)}, bf16[1,128,128]{2,1,0:T(8,128)(2,1)S(1)}) custom-call(bf16[24,64,512]{2,1,0:T(8,128)(2,1)} %q_hbm.1, bf16[24,64,512]{2,1,0:T(8,128)(2,1)} %g_hbm.1, bf16[1,128,128]{2,1,0:T(8,128)(2,1)} %k_hbm.1, bf16[1,128,128]{2,1,0:T(8,128)(2,1)} %v_hbm.1, ...), custom_call_target="tpu_custom_call" | custom-call | flops 2013265920 | bytes 4718592 | tf_op jit(solution)/shard_map/prefix_grads/pallas_call | solution.py:333
  30.4 1.2 %write_results.1 = (bf16[24,64,512]{2,1,0:T(8,128)(2,1)}, bf16[1,128,128]{2,1,0:T(8,128)(2,1)}, bf16[1,128,128]{2,1,0:T(8,128)(2,1)}) custom-call(bf16[24,64,512]{2,1,0:T(8,128)(2,1)S(1)} %get-tuple-element.6.dq_ref, bf16[1,128,128]{2,1,0:T(8,128)(2,1)S(1)} %get-tuple-element.7.kg_ref, bf16[1,128,128]{2,1,0:T(8,128)(2,1)S(1)} %get-tuple-element.8.vg_ref), custom_call_target="tpu_custom_call" | custom-call | tf_op jit(solution)/shard_map/write_results/pallas_call | solution.py:387

commit v10 on v9

--- a/solution.py
+++ b/solution.py
@@ -180,27 +180,34 @@
     def sib_copy(p):
         return remote(sib_out.at[p], sib_in.at[p], sib_send.at[p], sib_recv.at[p], sibling())
 
-    def par_copy(d):
-        return remote(par_out.at[d], par_in.at[d], par_send.at[d], par_recv.at[d], partner())
-
-    def line_copy(d):
-        return remote(line_out.at[d], line_in.at[d], line_send.at[d], line_recv.at[d], peer(d))
+    def par_copy(d, i):
+        return remote(
+            par_out.at[d, i], par_in.at[d, i], par_send.at[d, i], par_recv.at[d, i], partner()
+        )
+
+    def line_copy(d, i):
+        return remote(
+            line_out.at[d, i], line_in.at[d, i], line_send.at[d, i], line_recv.at[d, i], peer(d)
+        )
 
     def to_partner(d):
         p = along(d) * 2 + other
         sib_copy(p).wait_recv()
-        par_out[d] = (part[p] + sib_in[p].astype(f32)).astype(jnp.bfloat16)
-        par_copy(d).start()
-
-    def chip_sum(d):
+        for i in range(2):
+            par_out[d, i] = (part[p, i] + sib_in[p, i].astype(f32)).astype(jnp.bfloat16)
+            par_copy(d, i).start()
+
+    def chip_sum(d, i):
         p = along(d) * 2 + b
-        sib_copy(p).wait_recv()
-        par_copy(d).wait_recv()
-        return part[p] + sib_in[p].astype(f32) + par_in[d].astype(f32)
+        if i == 0:
+            sib_copy(p).wait_recv()
+        par_copy(d, i).wait_recv()
+        return part[p, i] + sib_in[p, i].astype(f32) + par_in[d, i].astype(f32)
 
     def to_owner(d):
-        line_out[d] = chip_sum(d).astype(jnp.bfloat16)
-        line_copy(d).start()
+        for i in range(2):
+            line_out[d, i] = chip_sum(d, i).astype(jnp.bfloat16)
+            line_copy(d, i).start()
 
     def forward_along(d):
         p = along(d) * 2 + b
@@ -269,7 +276,8 @@
 
     def drain(d, carry):
         kv_copy(along(d) * 2 + b, kv_par_send.at[d], partner()).wait_send()
-        par_copy(d).wait_send()
+        for i in range(2):
+            par_copy(d, i).wait_send()
         return carry
 
     def drain_prefix(p, carry):
@@ -282,14 +290,15 @@
         kv_copy(dp, kv_line_send.at[d], peer(d)).wait_send()
     lax.fori_loop(0, line, drain, 0)
     lax.fori_loop(0, prefixes, drain_prefix, 0)
-    total = chip_sum(0)
+    for i, grad_ref in enumerate((kg_ref, vg_ref)):
+        total = chip_sum(0, i)
+        for d in range(1, line):
+            line_copy(d, i).wait_recv()
+            total = total + line_in[d, i].astype(f32)
+        grad_ref[0] = total.astype(jnp.bfloat16)
     for d in range(1, line):
-        line_copy(d).wait_recv()
-        total = total + line_in[d].astype(f32)
-    kg_ref[0] = total[0].astype(jnp.bfloat16)
-    vg_ref[0] = total[1].astype(jnp.bfloat16)
-    for d in range(1, line):
-        line_copy(d).wait_send()
+        for i in range(2):
+            line_copy(d, i).wait_send()
 
 
 def write_kernel(dq_ref, kg_ref, vg_ref, dq_hbm, kg_hbm, vg_hbm, sem):
@@ -368,10 +377,10 @@
             dma((line,)),
             dma((prefixes,)),
             dma((prefixes,)),
-            dma((line,)),
-            dma((line,)),
-            dma((line,)),
-            dma((line,)),
+            dma((line, 2)),
+            dma((line, 2)),
+            dma((line, 2)),
+            dma((line, 2)),
         ],
         compiler_params=pltpu.CompilerParams(
             collective_id=0, has_side_effects=True, vmem_limit_bytes=48 << 20

time: 31.8 us -> 31.4 us (0.987)
  Pallas kernels: 31 us -> 30.6 us
    pallas_call x1, Pallas kernels: 29.8 us -> 29.4 us  [shards(): pl.pallas_call(functools.partial(exchange_kernel, cap), out_shape=(jax.Sh...]
where the time goes in v10:
time: 31.4 us; the launch traced here: 31.3 us
  Pallas kernels  30.6 us (97%)
  between operations  0.64 us (2%)
    pallas_call x1, Pallas kernels, shards(): pl.pallas_call(functools.partial(exchange_kernel, cap), out_shape=(jax.Sh...  29.4 us
    pallas_call x1, Pallas kernels, shards(): pl.pallas_call(write_kernel, out_shape=(jax.ShapeDtypeStruct(queries.shap...  1.24 us

profile of v10, /device:TPU:0, one launch (start us, length us, event | category | flops | bytes accessed | tf_op | source)
XLA Modules:
  0.0 31.3 jit_solution(5649376530192826455)
XLA Ops:
  0.6 29.4 %prefix_grads.1 = (bf16[24,64,512]{2,1,0:T(8,128)(2,1)S(1)}, bf16[1,128,128]{2,1,0:T(8,128)(2,1)S(1)}, bf16[1,128,128]{2,1,0:T(8,128)(2,1)S(1)}) custom-call(bf16[24,64,512]{2,1,0:T(8,128)(2,1)} %q_hbm.1, bf16[24,64,512]{2,1,0:T(8,128)(2,1)} %g_hbm.1, bf16[1,128,128]{2,1,0:T(8,128)(2,1)} %k_hbm.1, bf16[1,128,128]{2,1,0:T(8,128)(2,1)} %v_hbm.1, ...), custom_call_target="tpu_custom_call" | custom-call | flops 2013265920 | bytes 4718592 | tf_op jit(solution)/shard_map/prefix_grads/pallas_call | solution.py:342
  30.0 1.2 %write_results.1 = (bf16[24,64,512]{2,1,0:T(8,128)(2,1)}, bf16[1,128,128]{2,1,0:T(8,128)(2,1)}, bf16[1,128,128]{2,1,0:T(8,128)(2,1)}) custom-call(bf16[24,64,512]{2,1,0:T(8,128)(2,1)S(1)} %get-tuple-element.6.dq_ref, bf16[1,128,128]{2,1,0:T(8,128)(2,1)S(1)} %get-tuple-element.7.kg_ref, bf16[1,128,128]{2,1,0:T(8,128)(2,1)S(1)} %get-tuple-element.8.vg_ref), custom_call_target="tpu_custom_call" | custom-call | tf_op jit(solution)/shard_map/write_results/pallas_call | solution.py:396
